TPU v7x, 32 devices: a whole 2x2x4 slice. The times are simulated.
32 devices in a mesh: seq: 8 (over z, x), mlp: 4 (over y, core).
Axes of the slice: x: 2, y: 2, z: 4, core: 2. Of those that a mesh axis runs over, the one named last changes fastest.
Arguments:
- tokens: bfloat16 [12, 2048, 1024], P(None, 'seq'), may hold values from -6 to 6
- lengths: int32 [12, 8], replicated, may hold values from 1 to 2048, as said below
- counts: int32 [12], replicated, may hold values from 1 to 8
- norm_gain: float32 [1024], replicated, may hold values from 0.5 to 1.5
- norm_bias: float32 [1024], replicated, may hold values from -4 to 4
- head_weight: bfloat16 [3, 1024, 1024], P(None, None, 'mlp'), may hold values from -0.1875 to 0.1875
- merge_weight: bfloat16 [1024, 1024], P('mlp'), may hold values from -1.5 to 1.5
- up_weight: bfloat16 [1024, 4096], P(None, 'mlp'), may hold values from -0.1875 to 0.1875
- up_bias: float32 [4096], P('mlp'), may hold values from -6 to 6
- down_weight: bfloat16 [4096, 1024], P('mlp'), may hold values from -0.09375 to 0.09375
- down_bias: float32 [1024], replicated, may hold values from -6 to 6
- cotangent: bfloat16 [12, 2048, 1024], P(None, 'seq', 'mlp'), may hold values from -6 to 6
Outputs:
- result: bfloat16 [12, 2048, 1024], P(None, 'seq', 'mlp')
- tokens_grad: bfloat16 [12, 2048, 1024], P(None, 'seq')
- gain_grad: float32 [1024], P('seq')
- shift_grad: float32 [1024], P('seq')
- head_grad: float32 [3, 1024, 1024], P(None, 'seq', 'mlp')
- merge_grad: float32 [1024, 1024], P('mlp', 'seq')
- up_grad: float32 [1024, 4096], P('seq', 'mlp')
- up_bias_grad: float32 [4096], P(('mlp', 'seq'))
- down_grad: float32 [4096, 1024], P('mlp', 'seq')
- down_bias_grad: float32 [1024], P('seq')
Inputs may be any that keep to these rules, and one draw needn't show every extreme that they name: In row p the first counts[p] entries are the lengths of the proteins packed from position 0; they sum to at most 2048, and positions after them are padding. Later entries are to be ignored. In every draw one pack holds a single protein of 2048 residues.
All inputs are finite; a program needn't handle non-finite values.
Results may differ from a plain program's by a relative error of at most 0.011.
Values may be sent and summed in bfloat16 or wider, within the bound.
A program may use at most 320 MiB of HBM per device.

v0:
```python
import math

import jax
import jax.numpy as jnp
from jax import lax
from jax.sharding import PartitionSpec as P

HD = 64
ROT = 32


EPS = 1e-05
NEG = -1e30


def normalize(inputs, gain, shift):
    mean = jnp.mean(inputs, axis=-1, keepdims=True)
    cent = inputs - mean
    var = jnp.mean(cent * cent, axis=-1, keepdims=True)
    return cent * lax.rsqrt(var + EPS) * gain + shift


def rotate(values, place, rot):
    half = rot // 2
    freq = 10000.0 ** (-(2.0 * jnp.arange(half, dtype=jnp.float32)) / rot)
    angle = place.astype(jnp.float32)[..., None, None] * freq
    cosine = jnp.cos(angle)
    sine = jnp.sin(angle)
    pairs = values[..., :rot].reshape(values.shape[:-1] + (half, 2))
    first = pairs[..., 0]
    second = pairs[..., 1]
    turned = jnp.stack([first * cosine - second * sine, second * cosine + first * sine], axis=-1)
    return jnp.concatenate([turned.reshape(values.shape[:-1] + (rot,)), values[..., rot:]], axis=-1)


def layout(lengths, counts, pack_len):
    slots = lengths.shape[-1]
    slot_ids = jnp.arange(slots, dtype=jnp.int32)
    used = slot_ids[None, :] < counts[:, None]
    sizes = jnp.where(used, lengths, 0)
    ends = jnp.cumsum(sizes, axis=-1)
    starts = ends - sizes
    filled = ends[:, -1:]
    place = jnp.arange(pack_len, dtype=jnp.int32)[None, :]
    ended = jnp.sum(
        ((place[:, :, None] >= ends[:, None, :]) & used[:, None, :]).astype(jnp.int32), axis=-1
    )
    begin = jnp.sum(
        jnp.where(slot_ids[None, None, :] == ended[:, :, None], starts[:, None, :], 0), axis=-1
    )
    inside = place < filled
    segment = jnp.where(inside, ended, counts[:, None] + place)
    position = jnp.where(inside, place - begin, place - filled)
    return (segment, position)


def masked_scores(query, keys, seg_query, seg_keys, index_query, index_keys, scale):
    scores = jnp.einsum("gqhd,gkhd->ghqk", query, keys, preferred_element_type=jnp.float32) * scale
    allowed = (seg_query[:, :, None] == seg_keys[:, None, :]) & (
        index_keys[None, None, :] <= index_query[None, :, None]
    )
    return jnp.where(allowed[:, None], scores, NEG)


def on_device(
    tokens,
    lengths,
    counts,
    norm_gain,
    norm_bias,
    head_weight,
    merge_weight,
    up_weight,
    up_bias,
    down_weight,
    down_bias,
    cotangent,
):
    packs, shard, width = tokens.shape
    pack_len = shard * lax.axis_size("seq")
    rank = lax.axis_index("seq")
    heads_here = merge_weight.shape[0] // HD
    joined = heads_here * HD
    scale = 1.0 / math.sqrt(HD)
    limit = max(1, 1024 // shard)
    group = max((g for g in range(1, packs + 1) if packs % g == 0 and g <= limit))
    blocks = packs // group
    segment, position = layout(lengths, counts, pack_len)
    seg_own = lax.dynamic_slice_in_dim(segment, rank * shard, shard, 1)
    pos_own = lax.dynamic_slice_in_dim(position, rank * shard, shard, 1)
    own_rows = rank * shard + jnp.arange(shard, dtype=jnp.int32)
    every_row = jnp.arange(pack_len, dtype=jnp.int32)

    def split_heads(values):
        return values.reshape(values.shape[:-1] + (heads_here, HD))

    def by_block(values):
        return values.reshape((blocks, group) + values.shape[1:])

    def unblock(values):
        return values.reshape((packs,) + values.shape[2:])

    inputs = tokens.astype(jnp.float32)
    normed_low = normalize(inputs, norm_gain, norm_bias).astype(jnp.bfloat16)
    projected = jnp.einsum(
        "psd,jde->jpse", normed_low, head_weight, preferred_element_type=jnp.float32
    )
    query_pre = split_heads(projected[0])
    _, rot_back = jax.vjp(lambda values: rotate(values, pos_own, ROT), query_pre)
    query_low = rotate(query_pre, pos_own, ROT).astype(jnp.bfloat16)
    key_low = rotate(split_heads(projected[1]), pos_own, ROT).astype(jnp.bfloat16)
    value_low = split_heads(projected[2]).astype(jnp.bfloat16)
    key_pair = jnp.stack(
        [key_low.reshape(packs, shard, joined), value_low.reshape(packs, shard, joined)]
    )
    key_values = lax.all_gather(key_pair, "seq", axis=2, tiled=True)

    def forward_block(slices):
        query, keys, values, seg_query, seg_keys = slices
        scores = masked_scores(query, keys, seg_query, seg_keys, own_rows, every_row, scale)
        top = jnp.max(scores, axis=-1)
        expo = jnp.exp(scores - top[..., None])
        total = jnp.sum(expo, axis=-1)
        probs = expo / total[..., None]
        attended = jnp.einsum(
            "ghqk,gkhd->gqhd",
            probs.astype(jnp.bfloat16),
            values,
            preferred_element_type=jnp.float32,
        )
        return (attended, top, total)

    attended, top, total = lax.map(
        forward_block,
        (
            by_block(query_low),
            by_block(split_heads(key_values[0])),
            by_block(split_heads(key_values[1])),
            by_block(seg_own),
            by_block(segment),
        ),
    )
    attended_low = unblock(attended).reshape(packs, shard, joined).astype(jnp.bfloat16)
    top = unblock(top)
    total = unblock(total)
    hidden = (
        jnp.einsum("psd,df->psf", normed_low, up_weight, preferred_element_type=jnp.float32)
        + up_bias
    )
    active_low = jax.nn.gelu(hidden, approximate=True).astype(jnp.bfloat16)
    branch = jnp.einsum(
        "psh,hd->psd", attended_low, merge_weight, preferred_element_type=jnp.float32
    ) + jnp.einsum("psf,fd->psd", active_low, down_weight, preferred_element_type=jnp.float32)
    summed = lax.psum_scatter(branch, "mlp", scatter_dimension=2, tiled=True)
    cols = summed.shape[2]
    col_start = lax.axis_index("mlp") * cols
    result = (
        lax.dynamic_slice_in_dim(inputs, col_start, cols, 2)
        + summed
        + lax.dynamic_slice_in_dim(down_bias, col_start, cols, 0)
    ).astype(jnp.bfloat16)
    grad_low = lax.all_gather(cotangent, "mlp", axis=2, tiled=True)
    grad_full = grad_low.astype(jnp.float32)
    down_bias_grad = jnp.sum(grad_full, axis=(0, 1))
    down_grad = jnp.einsum("psf,psd->fd", active_low, grad_low, preferred_element_type=jnp.float32)
    merge_grad = jnp.einsum(
        "psh,psd->hd", attended_low, grad_low, preferred_element_type=jnp.float32
    )
    active_grad = jnp.einsum(
        "psd,fd->psf", grad_low, down_weight, preferred_element_type=jnp.float32
    )
    _, gelu_back = jax.vjp(lambda values: jax.nn.gelu(values, approximate=True), hidden)
    hidden_grad = gelu_back(active_grad)[0].astype(jnp.bfloat16)
    up_bias_grad = jnp.sum(hidden_grad.astype(jnp.float32), axis=(0, 1))
    up_grad = jnp.einsum("psd,psf->df", normed_low, hidden_grad, preferred_element_type=jnp.float32)
    normed_grad = jnp.einsum(
        "psf,df->psd", hidden_grad, up_weight, preferred_element_type=jnp.float32
    )
    attended_grad = split_heads(
        jnp.einsum(
            "psd,hd->psh", grad_low, merge_weight, preferred_element_type=jnp.float32
        ).astype(jnp.bfloat16)
    )
    keys_full = by_block(split_heads(key_values[0]))
    values_full = by_block(split_heads(key_values[1]))

    def query_side(query, keys, values, out_grad, seg_query, seg_keys, row_top, row_total):
        scores = masked_scores(query, keys, seg_query, seg_keys, own_rows, every_row, scale)
        probs = jnp.exp(scores - row_top[..., None]) / row_total[..., None]
        prob_grad = jnp.einsum(
            "gqhd,gkhd->ghqk", out_grad, values, preferred_element_type=jnp.float32
        )
        inner = jnp.sum(probs * prob_grad, axis=-1)
        score_grad = (probs * (prob_grad - inner[..., None])).astype(jnp.bfloat16)
        query_grad = (
            jnp.einsum("ghqk,gkhd->gqhd", score_grad, keys, preferred_element_type=jnp.float32)
            * scale
        )
        return (probs, score_grad, query_grad, inner)

    def local_block(slices):
        query, keys, values, out_grad, seg_query, seg_keys, row_top, row_total = slices
        probs, score_grad, query_grad, inner = query_side(
            query, keys, values, out_grad, seg_query, seg_keys, row_top, row_total
        )
        return (query_grad, inner)

    query_grad, inner = lax.map(
        local_block,
        (
            by_block(query_low),
            keys_full,
            values_full,
            by_block(attended_grad),
            by_block(seg_own),
            by_block(segment),
            by_block(top),
            by_block(total),
        ),
    )
    inner = unblock(inner)
    query_pair = jnp.stack(
        [query_low.reshape(packs, shard, joined), attended_grad.reshape(packs, shard, joined)]
    )
    query_all = lax.all_gather(query_pair, "seq", axis=2, tiled=True)
    top_all, total_all, inner_all = (
        lax.all_gather(top, "seq", axis=2, tiled=True),
        lax.all_gather(total, "seq", axis=2, tiled=True),
        lax.all_gather(inner, "seq", axis=2, tiled=True),
    )

    def key_block(slices):
        query, out_grad, keys, values, seg_query, seg_keys, row_top, row_total, row_inner = slices
        scores = masked_scores(query, keys, seg_query, seg_keys, every_row, own_rows, scale)
        probs = jnp.exp(scores - row_top[..., None]) / row_total[..., None]
        prob_grad = jnp.einsum(
            "gqhd,gkhd->ghqk", out_grad, values, preferred_element_type=jnp.float32
        )
        score_grad = (probs * (prob_grad - row_inner[..., None])).astype(jnp.bfloat16)
        key_part = (
            jnp.einsum("ghqk,gqhd->gkhd", score_grad, query, preferred_element_type=jnp.float32)
            * scale
        )
        value_part = jnp.einsum(
            "ghqk,gqhd->gkhd",
            probs.astype(jnp.bfloat16),
            out_grad,
            preferred_element_type=jnp.float32,
        )
        return (key_part, value_part)

    key_grad, value_grad = lax.map(
        key_block,
        (
            by_block(split_heads(query_all[0])),
            by_block(split_heads(query_all[1])),
            by_block(key_low),
            by_block(value_low),
            by_block(segment),
            by_block(seg_own),
            by_block(top_all),
            by_block(total_all),
            by_block(inner_all),
        ),
    )
    key_grad = unblock(key_grad)
    value_grad = unblock(value_grad).reshape(packs, shard, joined)
    query_grad = unblock(query_grad)
    query_back = rot_back(query_grad)[0].reshape(packs, shard, joined)
    key_back = rot_back(key_grad)[0].reshape(packs, shard, joined)
    head_grads_low = jnp.stack([query_back, key_back, value_grad]).astype(jnp.bfloat16)
    head_grad = jnp.einsum(
        "psd,jpse->jde", normed_low, head_grads_low, preferred_element_type=jnp.float32
    )
    normed_grad = normed_grad + jnp.einsum(
        "jpse,jde->psd", head_grads_low, head_weight, preferred_element_type=jnp.float32
    )
    normed_grad = lax.psum(normed_grad, "mlp")
    _, norm_back = jax.vjp(normalize, inputs, norm_gain, norm_bias)
    input_part, gain_grad, shift_grad = norm_back(normed_grad)
    tokens_grad = (grad_full + input_part).astype(jnp.bfloat16)
    (
        head_grad,
        merge_grad,
        up_grad,
        down_grad,
        up_bias_grad,
        down_bias_grad,
        gain_grad,
        shift_grad,
    ) = (
        lax.psum_scatter(head_grad, "seq", scatter_dimension=1, tiled=True),
        lax.psum_scatter(merge_grad, "seq", scatter_dimension=1, tiled=True),
        lax.psum_scatter(up_grad, "seq", scatter_dimension=0, tiled=True),
        lax.psum_scatter(down_grad, "seq", scatter_dimension=1, tiled=True),
        lax.psum_scatter(up_bias_grad, "seq", scatter_dimension=0, tiled=True),
        lax.psum_scatter(down_bias_grad, "seq", scatter_dimension=0, tiled=True),
        lax.psum_scatter(gain_grad, "seq", scatter_dimension=0, tiled=True),
        lax.psum_scatter(shift_grad, "seq", scatter_dimension=0, tiled=True),
    )
    return (
        result,
        tokens_grad,
        gain_grad,
        shift_grad,
        head_grad,
        merge_grad,
        up_grad,
        up_bias_grad,
        down_grad,
        down_bias_grad,
    )


def solution(mesh):
    in_specs = (
        P(None, "seq", None),
        P(),
        P(),
        P(),
        P(),
        P(None, None, "mlp"),
        P("mlp", None),
        P(None, "mlp"),
        P("mlp"),
        P("mlp", None),
        P(),
        P(None, "seq", "mlp"),
    )
    out_specs = (
        P(None, "seq", "mlp"),
        P(None, "seq", None),
        P("seq"),
        P("seq"),
        P(None, "seq", "mlp"),
        P("mlp", "seq"),
        P("seq", "mlp"),
        P(("mlp", "seq")),
        P("mlp", "seq"),
        P("seq"),
    )
    return jax.shard_map(
        on_device, mesh=mesh, in_specs=in_specs, out_specs=out_specs, check_vma=False
    )
```

profile of v0, /device:TPU:17, one launch (start us, length us, event | category | flops | bytes accessed | tf_op | source)
XLA Modules:
  0.0 1958.9 jit_solution(13847380963365446022)
XLA Ops:
  55.3 12.1 fusion.118
  75.3 19.2 convert_reduce_fusion.1
  106.4 435.0 %all-gather.4.cloned.1.call-done = bf16[2,12,2048,256]{2,3,0,1:T(8,128)(2,1)} async-done(((bf16[2,12,256,256]{2,3,0,1:T(8,128)(2,1)}), bf16[2,12,2048,256]{2,3,0,1:T(8,128)(2,1)}) %all-gather.4.cloned.1.call-update) | async-done | bytes 25165840 | tf_op jit(solution)/shard_map/all_gather | solution.py:116
  541.4 18.3 fusion.137
  561.0 148.7 %while.41 = (s32[]{:T(128)}, bf16[3,4,256,4,64]{2,4,3,1,0:T(8,128)(2,1)}, f32[3,4,4,256]{3,2,1,0:T(4,128)S(1)}, f32[3,4,4,256]{3,2,1,0:T(4,128)S(1)}, bf16[3,4,2...) while((s32[]{:T(128)}, ...), condition=%wide.region_8.9_spmd.clone, body=%wide.region_5.8_spmd.clone.sunk | while | flops 2252857600 | bytes 120324224 | solution.py:133
  563.1 15.8 fusion.169
  578.9 15.1 fusion.170
  594.0 16.5 fusion.171
  612.6 15.9 fusion.169
  628.5 15.1 fusion.170
  643.7 16.5 fusion.171
  662.2 15.7 fusion.169
  678.0 15.1 fusion.170
  693.1 16.7 fusion.171
  712.0 221.0 %while.42 = (s32[]{:T(128)}, f32[3,4,256,4,64]{2,3,4,1,0:T(4,128)}, f32[3,4,4,256]{3,2,1,0:T(4,128)S(1)}, bf16[3,4,2048,4,64]{2,4,3,1,0:T(8,128)(2,1)}, s32[3,4,...) while((s32[]{:T(128)}, f32[3,4,256,4,64]{2,3,4,1,0:T(4,128)}, ...), condition=%wide.region_12.13_spmd.clone, body=%wide.region_10.12_spmd.clone.sunk | while | flops 3301699840 | bytes 190071952 | solution.py:208
  714.2 18.3 fusion.175
  732.6 28.1 %multiply_reduce_fusion.5 = (f32[4,4,256]{2,1,0:T(4,128)S(1)}, f32[4,4,256,2048]{3,2,1,0:T(8,128)}) fusion(f32[4,4,256,2048]{3,2,1,0:T(8,128)} %fusion.175, f32[4,4,256]{2,1,0:T(4,128)S(1)} %get-tuple-element.701, f32[4,4,256]{2,1,0:T(4,128)S(1)} %get-tuple-element.702, bf16[3,4,2048,4,64]{2,4,3,1,0:T(8,128)(2,1)} %get-tuple-element.782, ...), kind=kOutput, calls=%fused_computation.33.clone.1 | convolution fusion | flops 1124069376 | bytes 73974784 | tf_op jit(solution)/shard_map/while/body/eval_jaxpr/gqhd,gkhd->ghqk/dot_general | solution.py:58
  760.7 23.6 %fusion.176 = f32[1,4,256,4,64]{2,4,3,1,0:T(8,128)S(1)} fusion(f32[4,4,256,2048]{3,2,1,0:T(8,128)} %get-tuple-element.703, f32[4,4,256,2048]{3,2,1,0:T(8,128)} %fusion.175, f32[4,4,256]{2,1,0:T(4,128)S(1)} %get-tuple-element.704, bf16[3,4,2048,4,64]{2,4,3,1,0:T(8,128)(2,1)} %get-tuple-element.782, s32[]{:T(128)} %get-tuple-element.766), kind=kOutput, calls=%fused_computation.47.clone.1 | convolution fusion | flops 1099169792 | bytes 72368640 | tf_op jit(solution)/shard_map/while/body/eval_jaxpr/ghqk,gkhd->gqhd/dot_general | solution.py:196
  788.1 18.3 fusion.175
  806.4 28.1 %multiply_reduce_fusion.5 = (f32[4,4,256]{2,1,0:T(4,128)S(1)}, f32[4,4,256,2048]{3,2,1,0:T(8,128)}) fusion(f32[4,4,256,2048]{3,2,1,0:T(8,128)} %fusion.175, f32[4,4,256]{2,1,0:T(4,128)S(1)} %get-tuple-element.701, f32[4,4,256]{2,1,0:T(4,128)S(1)} %get-tuple-element.702, bf16[3,4,2048,4,64]{2,4,3,1,0:T(8,128)(2,1)} %get-tuple-element.782, ...), kind=kOutput, calls=%fused_computation.33.clone.1 | convolution fusion | flops 1124069376 | bytes 73974784 | tf_op jit(solution)/shard_map/while/body/eval_jaxpr/gqhd,gkhd->ghqk/dot_general | solution.py:58
  834.4 23.4 %fusion.176 = f32[1,4,256,4,64]{2,4,3,1,0:T(8,128)S(1)} fusion(f32[4,4,256,2048]{3,2,1,0:T(8,128)} %get-tuple-element.703, f32[4,4,256,2048]{3,2,1,0:T(8,128)} %fusion.175, f32[4,4,256]{2,1,0:T(4,128)S(1)} %get-tuple-element.704, bf16[3,4,2048,4,64]{2,4,3,1,0:T(8,128)(2,1)} %get-tuple-element.782, s32[]{:T(128)} %get-tuple-element.766), kind=kOutput, calls=%fused_computation.47.clone.1 | convolution fusion | flops 1099169792 | bytes 72368640 | tf_op jit(solution)/shard_map/while/body/eval_jaxpr/ghqk,gkhd->gqhd/dot_general | solution.py:196
  861.6 18.1 fusion.175
  879.8 28.1 %multiply_reduce_fusion.5 = (f32[4,4,256]{2,1,0:T(4,128)S(1)}, f32[4,4,256,2048]{3,2,1,0:T(8,128)}) fusion(f32[4,4,256,2048]{3,2,1,0:T(8,128)} %fusion.175, f32[4,4,256]{2,1,0:T(4,128)S(1)} %get-tuple-element.701, f32[4,4,256]{2,1,0:T(4,128)S(1)} %get-tuple-element.702, bf16[3,4,2048,4,64]{2,4,3,1,0:T(8,128)(2,1)} %get-tuple-element.782, ...), kind=kOutput, calls=%fused_computation.33.clone.1 | convolution fusion | flops 1124069376 | bytes 73974784 | tf_op jit(solution)/shard_map/while/body/eval_jaxpr/gqhd,gkhd->ghqk/dot_general | solution.py:58
  907.8 23.5 %fusion.176 = f32[1,4,256,4,64]{2,4,3,1,0:T(8,128)S(1)} fusion(f32[4,4,256,2048]{3,2,1,0:T(8,128)} %get-tuple-element.703, f32[4,4,256,2048]{3,2,1,0:T(8,128)} %fusion.175, f32[4,4,256]{2,1,0:T(4,128)S(1)} %get-tuple-element.704, bf16[3,4,2048,4,64]{2,4,3,1,0:T(8,128)(2,1)} %get-tuple-element.782, s32[]{:T(128)} %get-tuple-element.766), kind=kOutput, calls=%fused_computation.47.clone.1 | convolution fusion | flops 1099169792 | bytes 72368640 | tf_op jit(solution)/shard_map/while/body/eval_jaxpr/ghqk,gkhd->gqhd/dot_general | solution.py:196
  933.0 22.6 %all_gather.23 = f32[12,4,2048]{2,1,0:T(4,128)S(1)} all-gather(f32[12,4,256]{2,1,0:T(4,128)S(1)} %bitcast.309), channel_id=1, replica_groups=mesh['seq'=8,'mlp'=4] {'seq'}, dimensions={2}, use_global_device_ids=true | all-gather | bytes 442368 | tf_op jit(solution)/shard_map/all_gather | solution.py:229
  955.6 89.5 %all_gather.21 = f32[12,4,2048]{2,1,0:T(4,128)} all-gather(f32[12,4,256]{2,1,0:T(4,128)S(1)} %bitcast.307), channel_id=1, replica_groups=mesh['seq'=8,'mlp'=4] {'seq'}, dimensions={2}, use_global_device_ids=true | all-gather | bytes 442368 | tf_op jit(solution)/shard_map/all_gather | solution.py:227
  1045.1 23.5 %all_gather.22 = f32[12,4,2048]{2,1,0:T(4,128)S(1)} all-gather(f32[12,4,256]{2,1,0:T(4,128)S(1)} %bitcast.308), channel_id=1, replica_groups=mesh['seq'=8,'mlp'=4] {'seq'}, dimensions={2}, use_global_device_ids=true | all-gather | bytes 442368 | tf_op jit(solution)/shard_map/all_gather | solution.py:228
  1072.9 17.9 fusion.136
  1094.4 154.9 %while.43 = (s32[]{:T(128)}, f32[3,4,256,4,64]{2,3,4,1,0:T(4,128)}, bf16[3,4,256,4,64]{2,4,3,1,0:T(8,128)(2,1)}, bf16[3,4,2048,4,64]{2,4,3,1,0:T(8,128)(2,1)}, s...) while((s32[]{:T(128)}, f32[3,4,256,4,64]{2,3,4,1,0:T(4,128)}, ...), condition=%wide.region_14.15_spmd.clone, body=%wide.region_13.14_spmd.clone.sunk | while | flops 4367056896 | bytes 135514400 | solution.py:252
  1097.7 16.1 exponential_divide_fusion.3
  1113.8 16.2 fusion.184
  1131.7 14.3 fusion.185
  1149.3 16.1 exponential_divide_fusion.3
  1165.4 16.2 fusion.184
  1183.4 14.3 fusion.185
  1201.0 16.1 exponential_divide_fusion.3
  1217.1 16.2 fusion.184
  1235.0 14.3 fusion.185
  1270.5 11.9 bitcast_add_fusion
  1313.3 13.9 convolution_bitcast_fusion.1
  1327.2 13.5 convolution_bitcast_fusion
  1358.1 163.6 %all-reduce.15.cloned.1.call-done = f32[12,256,1024]{2,1,0:T(8,128)} async-done(((f32[12,256,1024]{2,1,0:T(8,128)}), f32[12,256,1024]{2,1,0:T(8,128)}) %all-reduce.15.cloned.1.call-update) | async-done | bytes 12582928 | tf_op jit(solution)/shard_map/psum | solution.py:278
  1547.3 24.7 %all-reduce.12 = (f32[1024]{0:T(1024)S(1)}, f32[1024]{0:T(1024)S(1)}, f32[1024]{0:T(1024)S(1)}, f32[1024]{0:T(1024)S(1)}) all-reduce(f32[1024]{0:T(1024)S(1)} %get-tuple-element.365, f32[1024]{0:T(1024)S(1)} %get-tuple-element.367, f32[1024]{0:T(1024)S(1)} %copy-done.32, ...), channel_id=3, replica_groups=mesh['seq'=8,'mlp'=4] {'seq'}, use_global_device_ids=true, to_apply=%region_19.20.clone | all-reduce | flops 4096 | bytes 32768
  1574.4 25.3 %reduce-scatter.8.cloned.1.call-done = f32[3,128,256]{1,2,0:T(8,128)} async-done(((f32[3,1024,256]{1,2,0:T(8,128)}), f32[3,128,256]{1,2,0:T(8,128)}) %reduce-scatter.8.cloned.1.call-update) | async-done | bytes 393232 | tf_op jit(solution)/shard_map/reduce_scatter | solution.py:292
  1601.6 100.1 %reduce-scatter.6.cloned.1.call-done = f32[12,256,256]{2,1,0:T(8,128)} async-done(((f32[12,256,1024]{2,1,0:T(8,128)}), f32[12,256,256]{2,1,0:T(8,128)}) %reduce-scatter.6.cloned.1.call-update) | async-done | bytes 3145744 | tf_op jit(solution)/shard_map/reduce_scatter | solution.py:154
  1706.2 87.7 %reduce-scatter.12.cloned.1.call-done = f32[128,1024]{1,0:T(8,128)} async-done(((f32[1024,1024]{1,0:T(8,128)}), f32[128,1024]{1,0:T(8,128)}) %reduce-scatter.12.cloned.1.call-update) | async-done | bytes 524304 | tf_op jit(solution)/shard_map/reduce_scatter | solution.py:294
  1793.9 92.9 %reduce-scatter.14.cloned.1.call-done = f32[1024,128]{1,0:T(8,128)} async-done(((f32[1024,1024]{1,0:T(8,128)}), f32[1024,128]{1,0:T(8,128)}) %reduce-scatter.14.cloned.1.call-update) | async-done | bytes 524304 | tf_op jit(solution)/shard_map/reduce_scatter | solution.py:295
  1886.8 65.2 %reduce-scatter.10.cloned.1.call-done = f32[256,128]{1,0:T(8,128)} async-done(((f32[256,1024]{1,0:T(8,128)}), f32[256,128]{1,0:T(8,128)}) %reduce-scatter.10.cloned.1.call-update) | async-done | bytes 131088 | tf_op jit(solution)/shard_map/reduce_scatter | solution.py:293
  (279 shorter events, 214.1 us)
Async XLA Ops:
  7.2 68.2 %copy-start = (bf16[1024,1024]{1,0:T(8,128)(2,1)S(1)}, bf16[1024,1024]{1,0:T(8,128)(2,1)}, u32[]{:S(2)}) copy-start(bf16[1024,1024]{1,0:T(8,128)(2,1)} %param.27) | copy-start | bytes 6291460
  7.2 60.2 %all-gather.6.cloned.1.call-start = ((), (), s32[]{:S(2)}) async-start(), calls=%async_computation.7 | async-start | bytes 7864320 | tf_op jit(solution)/shard_map/all_gather | solution.py:162
  7.9 533.5 %all-gather.4.cloned.1.call-start = ((), (), s32[]{:S(2)}) async-start(), calls=%async_computation.5 | async-start | bytes 28311552 | tf_op jit(solution)/shard_map/all_gather | solution.py:116
  8.0 4.6 copy-start.1
  8.0 7.3 copy-start.28
  8.0 7.3 copy-start.35
  8.0 7.3 copy-start.36
  12.6 42.7 %copy-start.22 = (f32[12,256]{1,0:T(8,128)}, f32[12,256]{1,0:T(8,128)S(1)}, u32[]{:S(2)}) copy-start(f32[12,256]{1,0:T(8,128)S(1)} %broadcast_multiply_fusion) | copy-start | bytes 36868
  15.3 39.9 %copy-start.26 = (f32[12,256]{1,0:T(8,128)}, f32[12,256]{1,0:T(8,128)S(1)}, u32[]{:S(2)}) copy-start(f32[12,256]{1,0:T(8,128)S(1)} %fusion.132) | copy-start | bytes 36868
  35.2 6.5 copy-start.16
  35.2 6.5 copy-start.18
  35.2 6.5 copy-start.3
  43.7 1029.3 %all-gather.8.cloned.1.call-start = ((), (), s32[]{:S(2)}) async-start(), calls=%async_computation.8 | async-start | bytes 28311552 | tf_op jit(solution)/shard_map/all_gather | solution.py:225
  48.5 5.4 copy-start.5
  48.5 6.7 copy-start.33
  55.3 12.1 copy-start.20
  67.4 6.0 copy-start.8
  75.3 21.9 %copy-start.34 = (bf16[1024,1024]{1,0:T(8,128)(2,1)S(1)}, bf16[1024,1024]{1,0:T(8,128)(2,1)}, u32[]{:S(2)}) copy-start(bf16[1024,1024]{1,0:T(8,128)(2,1)} %param.25) | copy-start | bytes 6291460
  106.4 1415.3 %all-reduce.15.cloned.1.call-start = ((), (), s32[]{:S(2)}) async-start(), calls=%async_computation.9 | async-start | bytes 25165824 | tf_op jit(solution)/shard_map/psum | solution.py:278
  1094.4 19.4 copy-start.12
  1094.4 19.4 copy-start.14
  1131.7 14.3 copy-start.13
  1131.7 14.3 copy-start.15
  1146.0 19.4 copy-start.12
  1146.0 19.4 copy-start.14
  1183.4 14.3 copy-start.13
  1183.4 14.3 copy-start.15
  1197.7 19.4 copy-start.12
  1197.7 19.4 copy-start.14
  1235.0 14.3 copy-start.13
  1235.0 14.3 copy-start.15
  1249.3 4.0 copy-start.10
  1249.3 4.0 copy-start.17
  1282.5 12.2 copy-start.39
  1282.5 317.2 %reduce-scatter.8.cloned.1.call-start = ((), (), s32[]{:S(2)}) async-start(), calls=%async_computation.10 | async-start | bytes 3538944 | tf_op jit(solution)/shard_map/reduce_scatter | solution.py:292
  1294.6 10.8 copy-start.21
  1294.6 407.1 %reduce-scatter.6.cloned.1.call-start = ((), (), s32[]{:S(2)}) async-start(), calls=%async_computation.6 | async-start | bytes 15728640 | tf_op jit(solution)/shard_map/reduce_scatter | solution.py:154
  1313.2 480.7 %reduce-scatter.12.cloned.1.call-start = ((), (), s32[]{:S(2)}) async-start(), calls=%async_computation.12 | async-start | bytes 4718592 | tf_op jit(solution)/shard_map/reduce_scatter | solution.py:294
  1327.2 559.6 %reduce-scatter.14.cloned.1.call-start = ((), (), s32[]{:S(2)}) async-start(), calls=%async_computation.13 | async-start | bytes 4718592 | tf_op jit(solution)/shard_map/reduce_scatter | solution.py:295
  1340.7 611.2 %reduce-scatter.10.cloned.1.call-start = ((), (), s32[]{:S(2)}) async-start(), calls=%async_computation.11 | async-start | bytes 1179648 | tf_op jit(solution)/shard_map/reduce_scatter | solution.py:293
  1340.8 9.0 copy-start.40
  1358.1 172.5 %copy-start.25 = (f32[12,256]{1,0:T(8,128)S(1)}, f32[12,256]{1,0:T(8,128)}, u32[]{:S(2)}) copy-start(f32[12,256]{1,0:T(8,128)} %copy-done.24) | copy-start | bytes 36868
  1521.7 10.0 copy-start.2
  1521.7 18.7 slice-start
  1521.7 18.8 slice-start.2
  1531.7 8.7 slice-start.1
  1531.7 8.8 slice-start.3
  1540.5 6.9 copy-start.32
  (15 other events, 35.9 us)
Sparse Core Ops, SparseCore 0:
  9.6 48.6 all-gather.5
  59.8 481.5 all-gather.3
  542.9 493.4 all-gather.7
  1282.6 239.0 all-reduce.14
  1525.1 74.5 reduce-scatter.7
  1602.2 99.5 reduce-scatter.5
  1706.0 87.8 reduce-scatter.11
  1798.5 88.2 reduce-scatter.13
  1890.8 61.1 reduce-scatter.9
where the time goes:
time: 1970 us; the launch traced here: 1960 us
  waiting for transfers between devices  971 us (49%)
  matrix products  573 us (29%)
  blocking collectives  160 us (8%)
  other arithmetic  131 us (7%)
  local copies, waits for them, and re-layouts  107 us (5%)
    all_gather x1, waiting for transfers between devices, on_device(): key_values = lax.all_gather(key_pair, 'seq', axis=2, tiled=True)  435 us
    dot_general x9, matrix products, masked_scores(): jnp.einsum('gqhd,gkhd->ghqk', query, keys, preferred_element_type=jnp.flo...  180 us
    psum x1, waiting for transfers between devices, on_device(): normed_grad = lax.psum(normed_grad, 'mlp')  164 us
    reduce_scatter x1, waiting for transfers between devices, on_device(): summed = lax.psum_scatter(branch, 'mlp', scatter_dimension=2, tiled=True)  100 us
    reduce_scatter x1, waiting for transfers between devices, on_device(): lax.psum_scatter(down_grad, 'seq', scatter_dimension=1, tiled=True)  92.9 us
    all_gather x1, blocking collectives, on_device(): lax.all_gather(top, 'seq', axis=2, tiled=True)  89.5 us
    reduce_scatter x1, waiting for transfers between devices, on_device(): lax.psum_scatter(up_grad, 'seq', scatter_dimension=0, tiled=True)  87.7 us
    dot_general x3, matrix products, query_side(): jnp.einsum('ghqk,gkhd->gqhd', score_grad, keys, preferred_element_type=jn...  70.5 us
  transfers between devices with their start and end apart: 9, of which 7 were waited for; matrix products, arithmetic and copies ran while one was open for 30% of the time, Pallas kernels for 0%

commit v1 on v0

v1 whole, which is shorter than its diff:
```python
import functools
import math

import jax
import jax.numpy as jnp
from jax import lax
from jax.experimental import pallas as pl
from jax.experimental.pallas import tpu as pltpu
from jax.sharding import PartitionSpec as P

HD = 64
ROT = 32
EPS = 1e-05
NEG = -1e30
BF16 = jnp.bfloat16
F32 = jnp.float32
VMEM_LIMIT = 56 * 1024 * 1024


def dot(a, b, dims=((1,), (0,))):
    return lax.dot_general(a, b, (dims, ((), ())), preferred_element_type=F32)


def layout(lengths, counts, pack_len):
    slots = lengths.shape[-1]
    slot_ids = jnp.arange(slots, dtype=jnp.int32)
    used = slot_ids[None, :] < counts[:, None]
    sizes = jnp.where(used, lengths, 0)
    ends = jnp.cumsum(sizes, axis=-1)
    starts = ends - sizes
    filled = ends[:, -1:]
    place = jnp.arange(pack_len, dtype=jnp.int32)[None, :]
    begin = jnp.max(
        jnp.where(used[:, None, :] & (place[:, :, None] >= starts[:, None, :]), starts[:, None, :], 0),
        axis=-1,
    )
    inside = place < filled
    first = jnp.where(inside, begin, place)
    position = jnp.where(inside, place - begin, place - filled)
    cost = jnp.sum(sizes * sizes, axis=-1)
    return first, position, cost


def turn(values, cosine, sine, heads):
    out = []
    parity = lax.broadcasted_iota(jnp.int32, cosine.shape, 0) % 2
    for h in range(heads):
        part = values[h * HD : h * HD + ROT]
        ahead = jnp.concatenate([part[1:], part[:1]], axis=0)
        behind = jnp.concatenate([part[-1:], part[:-1]], axis=0)
        swapped = jnp.where(parity == 0, -ahead, behind)
        out.append(part * cosine + swapped * sine)
        out.append(values[h * HD + ROT : (h + 1) * HD])
    return jnp.concatenate(out, axis=0)


def head_kernel(n, heads, me_ref, pack_ref, x_ref, gain_ref, bias_ref, w_ref, cos_ref, sin_ref, *refs):
    normed_ref, outs, scr = refs[0], refs[1 : 1 + n], refs[1 + n]
    g = pl.program_id(1)
    me = me_ref[0]
    width = heads * HD
    x = x_ref[0].astype(F32)
    cent = x - jnp.mean(x, axis=-1, keepdims=True)
    var = jnp.mean(cent * cent, axis=-1, keepdims=True)
    normed = (cent * lax.rsqrt(var + EPS) * gain_ref[...] + bias_ref[...]).astype(BF16)
    normed_ref[0] = normed
    for j in range(3):
        part = dot(w_ref[j * width : (j + 1) * width, :], normed, ((1,), (1,)))
        if j < 2:
            part = turn(part, cos_ref[0], sin_ref[0], heads)
        if j == 0:
            part = part * (1.0 / math.sqrt(HD))
        part = part.astype(BF16)
        for h in range(heads):
            scr[h, j] = part[h * HD : (h + 1) * HD]
    for k in range(n):
        d = lax.bitwise_xor(jnp.int32(k), me)

        @pl.when(d // heads == g)
        def _():
            outs[k][0] = scr[d % heads]


def grad_kernel(n, heads, me_ref, pack_ref, c_ref, w_ref, *refs):
    outs, scr = refs[:n], refs[n]
    g = pl.program_id(1)
    me = me_ref[0]
    part = dot(w_ref[...], c_ref[0], ((1,), (1,))).astype(BF16)
    for h in range(heads):
        scr[h] = part[h * HD : (h + 1) * HD]
    for k in range(n):
        d = lax.bitwise_xor(jnp.int32(k), me)

        @pl.when(d // heads == g)
        def _():
            outs[k][0] = scr[d % heads]


def attend_kernel(n, block, me_ref, pack_ref, low_ref, first_ref, *refs):
    qkv, grads, outs = refs[:n], refs[n : 2 * n], refs[2 * n : 3 * n]
    qt, kt, vt, gt, qn, kn, vn, gn, dk, dv, res = refs[3 * n :]
    s_id = pl.program_id(0)
    me = me_ref[0]
    for k in range(n):
        d = lax.bitwise_xor(jnp.int32(k), me)
        for j, (t_ref, n_ref) in enumerate(((qt, qn), (kt, kn), (vt, vn), (gt, gn))):
            part = qkv[k][0, j] if j < 3 else grads[k][0]
            t_ref[d] = part
            n_ref[d] = part.T
    dk[...] = jnp.zeros_like(dk)
    dv[...] = jnp.zeros_like(dv)
    rows = lax.broadcasted_iota(jnp.int32, (block, block), 0)
    cols = lax.broadcasted_iota(jnp.int32, (block, block), 1)
    ahead = rows - cols

    def outer(i, carry):
        q_t, g_t, q_n, g_n = qt[i], gt[i], qn[i], gn[i]
        first = first_ref[0, pl.ds(i, 1), :]
        j0 = low_ref[s_id, i]

        def scores(j):
            s = dot(kn[j], q_t)
            allowed = (rows >= first - j * block) & (ahead <= (i - j) * block)
            return jnp.where(allowed, s, NEG)

        def forward(j, state):
            top, total, acc = state
            s = scores(j)
            new_top = jnp.maximum(top, jnp.max(s, axis=0, keepdims=True))
            p = jnp.exp(s - new_top)
            fade = jnp.exp(top - new_top)
            total = total * fade + jnp.sum(p, axis=0, keepdims=True)
            acc = acc * fade + dot(vt[j], p.astype(BF16))
            return new_top, total, acc

        top, total, acc = lax.fori_loop(
            j0,
            i + 1,
            forward,
            (
                jnp.full((1, block), NEG, F32),
                jnp.zeros((1, block), F32),
                jnp.zeros((HD, block), F32),
            ),
        )
        acc = acc / total
        logsum = top + jnp.log(total)
        inner = jnp.sum(acc * g_t.astype(F32), axis=0, keepdims=True)
        res[i, 0] = acc.astype(BF16)

        def backward(j, dq):
            p = jnp.exp(scores(j) - logsum)
            dp = dot(vn[j], g_t)
            ds = (p * (dp - inner)).astype(BF16)
            dk[j] += dot(ds, q_n)
            dv[j] += dot(p.astype(BF16), g_n)
            return dq + dot(kt[j], ds)

        dq = lax.fori_loop(j0, i + 1, backward, jnp.zeros((HD, block), F32))
        res[i, 1] = (dq * (1.0 / math.sqrt(HD))).astype(BF16)
        return carry

    lax.fori_loop(0, n, outer, 0)
    for i in range(n):
        res[i, 2] = dk[i].T.astype(BF16)
        res[i, 3] = dv[i].T.astype(BF16)
    for k in range(n):
        d = lax.bitwise_xor(jnp.int32(k), me)
        outs[k][0] = res[d]


def close_kernel(n, heads, slices, me_ref, pack_ref, *refs):
    recv = refs[:n]
    normed_ref, c_ref, w_ref, merge_ref, cos_ref, sin_ref, branch_ref, low_ref = refs[n : n + 8]
    out_branch, out_low, out_weight, scr, acc = refs[n + 8 :]
    s_id, g = pl.program_id(0), pl.program_id(1)
    groups = pl.num_programs(1)
    me = me_ref[0]
    width = heads * HD
    shard = normed_ref.shape[1]

    @pl.when((s_id == 0) & (g == 0))
    def _():
        acc[...] = jnp.zeros_like(acc)

    for k in range(n):
        d = lax.bitwise_xor(jnp.int32(k), me)

        @pl.when(d // heads == g)
        def _():
            for j in range(4):
                scr[j, d % heads] = recv[k][0, j]

    @pl.when(pack_ref[g, s_id] < pack_ref[groups, 0])
    def _():
        attended = scr[0].reshape(width, shard)
        parts = []
        for j in (1, 2):
            part = scr[j].reshape(width, shard).astype(F32)
            parts.append(turn(part, cos_ref[0], -sin_ref[0], heads).astype(BF16))
        parts.append(scr[3].reshape(width, shard))
        grads = jnp.concatenate(parts, axis=0)
        acc[: 3 * width] += dot(grads, normed_ref[0])
        acc[3 * width :] += dot(attended, c_ref[0])
        low = dot(grads.T, w_ref[...]) + low_ref[0].astype(F32)
        out_low[0] = low.astype(BF16)
        branch = dot(attended.T, merge_ref[...]) + branch_ref[0].astype(F32)
        cols = branch.shape[1] // slices
        for m in range(slices):
            out_branch[m, 0] = branch[:, m * cols : (m + 1) * cols].astype(BF16)

    @pl.when((s_id == pl.num_programs(0) - 1) & (g == groups - 1))
    def _():
        out_weight[...] = acc[...].astype(BF16)


def params():
    return pltpu.CompilerParams(vmem_limit_bytes=VMEM_LIMIT)


def swap(parts):
    out = [parts[0]]
    n = len(parts)
    for k in range(1, n):
        out.append(lax.ppermute(parts[k], "seq", [(i, i ^ k) for i in range(n)]))
    return out


def on_device(
    tokens,
    lengths,
    counts,
    norm_gain,
    norm_bias,
    head_weight,
    merge_weight,
    up_weight,
    up_bias,
    down_weight,
    down_bias,
    cotangent,
):
    packs, shard, width = tokens.shape
    n = lax.axis_size("seq")
    slices = lax.axis_size("mlp")
    pack_len = shard * n
    rank = lax.axis_index("seq")
    column = lax.axis_index("mlp")
    heads = merge_weight.shape[0] // HD
    joined = heads * HD
    groups = n // heads
    slots = -(-packs // groups)
    spare = 1 if groups * slots > packs else 0
    rows = packs * shard

    cot = lax.all_gather(cotangent, "mlp", axis=2, tiled=True)

    first, position, cost = layout(lengths, counts, pack_len)
    ids = jnp.arange(packs, dtype=jnp.int32)
    before = (cost[None, :] > cost[:, None]) | (
        (cost[None, :] == cost[:, None]) & (ids[None, :] < ids[:, None])
    )
    order = jnp.sum(before.astype(jnp.int32), axis=1)
    slot_of = order // groups
    group_of = jnp.where(slot_of % 2 == 0, order % groups, groups - 1 - order % groups)
    hit = (group_of[None, None, :] == jnp.arange(groups)[:, None, None]) & (
        slot_of[None, None, :] == jnp.arange(slots)[None, :, None]
    )
    pack_at = jnp.where(
        jnp.any(hit, axis=-1), jnp.sum(jnp.where(hit, ids, 0), axis=-1), packs
    ).astype(jnp.int32)
    pack_table = jnp.concatenate([pack_at, jnp.full((1, slots), packs, jnp.int32)], axis=0)
    me = rank.astype(jnp.int32).reshape(1)

    half = ROT // 2
    freq = 10000.0 ** (-(2.0 * jnp.arange(half, dtype=F32)) / ROT)
    own_position = lax.dynamic_slice_in_dim(position, rank * shard, shard, 1)
    angle = own_position.astype(F32)[:, None, :] * jnp.repeat(freq, 2)[None, :, None]
    cosine, sine = jnp.cos(angle), jnp.sin(angle)

    w_t = jnp.transpose(head_weight, (0, 2, 1)).reshape(3 * joined, width)

    def pack_in(s, g, me_ref, pack_ref):
        return (jnp.minimum(pack_ref[g, s], packs - 1), 0, 0)

    def pack_out(s, g, me_ref, pack_ref):
        return (pack_ref[g, s], 0, 0)

    def whole2(s, g, me_ref, pack_ref):
        return (0, 0)

    row_spec = pl.BlockSpec((1, shard, width), pack_in)
    table_spec = pl.BlockSpec((1, ROT, shard), pack_in)
    outs = pl.pallas_call(
        functools.partial(head_kernel, n, heads),
        grid_spec=pltpu.PrefetchScalarGridSpec(
            num_scalar_prefetch=2,
            grid=(slots, groups),
            in_specs=[
                row_spec,
                pl.BlockSpec((1, width), whole2),
                pl.BlockSpec((1, width), whole2),
                pl.BlockSpec((3 * joined, width), whole2),
                table_spec,
                table_spec,
            ],
            out_specs=[pl.BlockSpec((1, shard, width), pack_out)]
            + [pl.BlockSpec((1, 3, HD, shard), lambda s, g, a, b: (s, 0, 0, 0))] * n,
            scratch_shapes=[pltpu.VMEM((heads, 3, HD, shard), BF16)],
        ),
        out_shape=[jax.ShapeDtypeStruct((packs + spare, shard, width), BF16)]
        + [jax.ShapeDtypeStruct((slots, 3, HD, shard), BF16)] * n,
        compiler_params=params(),
        cost_estimate=pl.CostEstimate(
            flops=2 * rows * width * 3 * joined,
            bytes_accessed=rows * width * 4 + rows * joined * 6,
            transcendentals=0,
        ),
        name="heads",
    )(
        me,
        pack_table,
        tokens,
        norm_gain.reshape(1, width),
        norm_bias.reshape(1, width),
        w_t,
        cosine,
        sine,
    )
    normed_low = outs[0][:packs]
    qkv = swap(outs[1:])

    sends = pl.pallas_call(
        functools.partial(grad_kernel, n, heads),
        grid_spec=pltpu.PrefetchScalarGridSpec(
            num_scalar_prefetch=2,
            grid=(slots, groups),
            in_specs=[row_spec, pl.BlockSpec((joined, width), whole2)],
            out_specs=[pl.BlockSpec((1, HD, shard), lambda s, g, a, b: (s, 0, 0))] * n,
            scratch_shapes=[pltpu.VMEM((heads, HD, shard), BF16)],
        ),
        out_shape=[jax.ShapeDtypeStruct((slots, HD, shard), BF16)] * n,
        compiler_params=params(),
        cost_estimate=pl.CostEstimate(
            flops=2 * rows * width * joined,
            bytes_accessed=rows * width * 2 + rows * joined * 2,
            transcendentals=0,
        ),
        name="out_grads",
    )(me, pack_table, cot, merge_weight)
    grads = swap(sends)

    hidden = (
        jnp.einsum("psd,df->psf", normed_low, up_weight, preferred_element_type=F32) + up_bias
    )
    active_low = jax.nn.gelu(hidden, approximate=True).astype(BF16)
    active_grad = jnp.einsum("psd,fd->psf", cot, down_weight, preferred_element_type=F32)
    _, gelu_back = jax.vjp(lambda values: jax.nn.gelu(values, approximate=True), hidden)
    hidden_grad = gelu_back(active_grad)[0].astype(BF16)
    up_bias_grad = jnp.sum(hidden_grad.astype(F32), axis=(0, 1))
    down_bias_grad = jnp.sum(cot.astype(F32), axis=(0, 1))
    branch_ff = jnp.einsum(
        "psf,fd->psd", active_low, down_weight, preferred_element_type=F32
    ).astype(BF16)
    low_ff = jnp.einsum(
        "psf,df->psd", hidden_grad, up_weight, preferred_element_type=F32
    ).astype(BF16)
    up_grad = jnp.einsum(
        "psd,psf->df", normed_low, hidden_grad, preferred_element_type=F32
    ).astype(BF16)
    down_grad = jnp.einsum("psd,psf->df", cot, active_low, preferred_element_type=F32).astype(BF16)
    up_grad = lax.psum_scatter(up_grad, "seq", scatter_dimension=0, tiled=True)
    down_grad = lax.psum_scatter(down_grad, "seq", scatter_dimension=0, tiled=True)

    my_packs = lax.dynamic_slice_in_dim(pack_at, rank // heads, 1, 0)[0]
    safe = jnp.minimum(my_packs, packs - 1)
    lows = first.reshape(packs, n, shard)[:, :, 0] // shard
    lows = jnp.where((my_packs < packs)[:, None], lows[safe], jnp.arange(n)[None, :]).astype(
        jnp.int32
    )
    chunk_spec = pl.BlockSpec((1, 3, HD, shard), lambda s, a, b, c: (s, 0, 0, 0))
    grad_spec = pl.BlockSpec((1, HD, shard), lambda s, a, b, c: (s, 0, 0))
    backs = pl.pallas_call(
        functools.partial(attend_kernel, n, shard),
        grid_spec=pltpu.PrefetchScalarGridSpec(
            num_scalar_prefetch=3,
            grid=(slots,),
            in_specs=[pl.BlockSpec((1, n, shard), lambda s, a, b, c: (b[s], 0, 0))]
            + [chunk_spec] * n
            + [grad_spec] * n,
            out_specs=[pl.BlockSpec((1, 4, HD, shard), lambda s, a, b, c: (s, 0, 0, 0))] * n,
            scratch_shapes=[pltpu.VMEM((n, HD, shard), BF16)] * 4
            + [pltpu.VMEM((n, shard, HD), BF16)] * 4
            + [pltpu.VMEM((n, shard, HD), F32)] * 2
            + [pltpu.VMEM((n, 4, HD, shard), BF16)],
        ),
        out_shape=[jax.ShapeDtypeStruct((slots, 4, HD, shard), BF16)] * n,
        compiler_params=params(),
        cost_estimate=pl.CostEstimate(
            flops=slots * pack_len * pack_len * HD * 14,
            bytes_accessed=slots * pack_len * HD * 16,
            transcendentals=slots * pack_len * pack_len,
        ),
        name="attend",
    )(me, safe, lows, first.reshape(packs, n, shard), *qkv, *grads)
    backs = swap(backs)

    branch, low, weight = pl.pallas_call(
        functools.partial(close_kernel, n, heads, slices),
        grid_spec=pltpu.PrefetchScalarGridSpec(
            num_scalar_prefetch=2,
            grid=(slots, groups),
            in_specs=[pl.BlockSpec((1, 4, HD, shard), lambda s, g, a, b: (s, 0, 0, 0))] * n
            + [
                row_spec,
                row_spec,
                pl.BlockSpec((3 * joined, width), whole2),
                pl.BlockSpec((joined, width), whole2),
                table_spec,
                table_spec,
                row_spec,
                row_spec,
            ],
            out_specs=[
                pl.BlockSpec(
                    (slices, 1, shard, width // slices), lambda s, g, a, b: (0, b[g, s], 0, 0)
                ),
                pl.BlockSpec((1, shard, width), pack_out),
                pl.BlockSpec((4 * joined, width), whole2),
            ],
            scratch_shapes=[
                pltpu.VMEM((4, heads, HD, shard), BF16),
                pltpu.VMEM((4 * joined, width), F32),
            ],
        ),
        out_shape=[
            jax.ShapeDtypeStruct((slices, packs + spare, shard, width // slices), BF16),
            jax.ShapeDtypeStruct((packs + spare, shard, width), BF16),
            jax.ShapeDtypeStruct((4 * joined, width), BF16),
        ],
        compiler_params=params(),
        cost_estimate=pl.CostEstimate(
            flops=16 * rows * width * joined,
            bytes_accessed=rows * width * 12 + rows * joined * 8,
            transcendentals=0,
        ),
        name="close",
    )(
        me,
        pack_table,
        *backs,
        normed_low,
        cot,
        w_t,
        merge_weight,
        cosine,
        sine,
        branch_ff,
        low_ff,
    )
    branch = branch[:, :packs]
    low = low[:packs]
    summed = lax.psum_scatter(branch, "mlp", scatter_dimension=0, tiled=False)
    cols = width // slices
    result = (
        lax.dynamic_slice_in_dim(tokens, column * cols, cols, 2).astype(F32)
        + summed.astype(F32)
        + lax.dynamic_slice_in_dim(down_bias, column * cols, cols, 0)
    ).astype(BF16)

    share = rows // slices
    low_sum = lax.psum_scatter(
        low.reshape(rows, width), "mlp", scatter_dimension=0, tiled=True
    ).astype(F32)
    row_in = lax.dynamic_slice_in_dim(
        tokens.reshape(rows, width), column * share, share, 0
    ).astype(F32)
    row_cot = lax.dynamic_slice_in_dim(
        cot.reshape(rows, width), column * share, share, 0
    ).astype(F32)
    cent = row_in - jnp.mean(row_in, axis=-1, keepdims=True)
    inverse = lax.rsqrt(jnp.mean(cent * cent, axis=-1, keepdims=True) + EPS)
    xhat = cent * inverse
    g = low_sum * norm_gain
    row_grad = (
        row_cot
        + (
            g
            - jnp.mean(g, axis=-1, keepdims=True)
            - xhat * jnp.mean(g * xhat, axis=-1, keepdims=True)
        )
        * inverse
    ).astype(BF16)
    tokens_grad = lax.all_gather(row_grad, "mlp", axis=0, tiled=True).reshape(packs, shard, width)
    gain_grad = lax.psum(jnp.sum(low_sum * xhat, axis=0), "mlp")
    shift_grad = lax.psum(jnp.sum(low_sum, axis=0), "mlp")

    weight = lax.psum_scatter(weight, "seq", scatter_dimension=1, tiled=True).astype(F32)
    part = width // n
    head_grad = jnp.transpose(weight[: 3 * joined].reshape(3, joined, part), (0, 2, 1))
    merge_grad = weight[3 * joined :]
    gain_grad, shift_grad, up_bias_grad, down_bias_grad = (
        lax.psum_scatter(gain_grad, "seq", scatter_dimension=0, tiled=True),
        lax.psum_scatter(shift_grad, "seq", scatter_dimension=0, tiled=True),
        lax.psum_scatter(up_bias_grad, "seq", scatter_dimension=0, tiled=True),
        lax.psum_scatter(down_bias_grad, "seq", scatter_dimension=0, tiled=True),
    )
    return (
        result,
        tokens_grad,
        gain_grad,
        shift_grad,
        head_grad,
        merge_grad,
        up_grad.astype(F32),
        up_bias_grad,
        down_grad.astype(F32).T,
        down_bias_grad,
    )


def solution(mesh):
    in_specs = (
        P(None, "seq", None),
        P(),
        P(),
        P(),
        P(),
        P(None, None, "mlp"),
        P("mlp", None),
        P(None, "mlp"),
        P("mlp"),
        P("mlp", None),
        P(),
        P(None, "seq", "mlp"),
    )
    out_specs = (
        P(None, "seq", "mlp"),
        P(None, "seq", None),
        P("seq"),
        P("seq"),
        P(None, "seq", "mlp"),
        P("mlp", "seq"),
        P("seq", "mlp"),
        P(("mlp", "seq")),
        P("mlp", "seq"),
        P("seq"),
    )
    return jax.shard_map(
        on_device, mesh=mesh, in_specs=in_specs, out_specs=out_specs, check_vma=False
    )
```

time: 1970 us -> 879 us (0.45)
  waiting for transfers between devices: 971 us -> 469 us
  matrix products: 573 us -> 74.3 us
  Pallas kernels: 0 us -> 162 us
  blocking collectives: 160 us -> 38 us
  other arithmetic: 131 us -> 27.7 us
  local copies, waits for them, and re-layouts: 107 us -> 30.4 us
  starting transfers between devices: 0.37 us -> 48 us
    dot_general x33 -> x3, matrix products: 540 us -> 40.5 us  [the longest x1 19.6 us: on_device(): jnp.einsum('psd,fd->psf', cot, down_weight, preferred_element_type=F32)]
    all_gather x3 -> x2, waiting for transfers between devices: 435 us -> 44.9 us  [the longest x1 44.9 us: on_device(): lax.all_gather(row_grad, 'mlp', axis=0, tiled=True)]
    reduce_scatter x5 -> x3, waiting for transfers between devices: 371 us -> 115 us  [the longest x1 69.1 us: on_device(): up_grad = lax.psum_scatter(up_grad, 'seq', scatter_dimension=0, tiled=True)]
    ppermute x0 -> x21, waiting for transfers between devices: none -> 183 us  [swap(): out.append(lax.ppermute(parts[k], 'seq', [(i, i ^ k) for i in range(n)]))]
    psum x1 -> x0, waiting for transfers between devices: 164 us -> none  [on_device(): normed_grad = lax.psum(normed_grad, 'mlp')]
    pallas_call x0 -> x4, Pallas kernels: none -> 162 us  [the longest x1 104 us: on_device(): pl.pallas_call(functools.partial(attend_kernel, n, shard), grid_spec=pltp...]
    all_gather x3 -> x0, blocking collectives: 136 us -> none  [the longest x1 89.5 us: on_device(): lax.all_gather(top, 'seq', axis=2, tiled=True)]
    unnamed x9, waiting for transfers between devices: 0.81 us -> 126 us
  transfers between devices with their start and end apart: 9 -> 28, of which waited for: 7 -> 17; matrix products, arithmetic and copies ran while one was open for 30% -> 14% of each run, Pallas kernels for 0% -> 4%
where the time goes in v1:
time: 879 us; the launch traced here: 865 us
  waiting for transfers between devices  469 us (53%)
  Pallas kernels  162 us (18%)
  matrix products  74.3 us (8%)
  starting transfers between devices  48 us (5%)
  blocking collectives  38 us (4%)
  local copies, waits for them, and re-layouts  30.4 us (3%)
  other arithmetic  27.7 us (3%)
  between operations  15.7 us (2%)
    ppermute x21, waiting for transfers between devices, swap(): out.append(lax.ppermute(parts[k], 'seq', [(i, i ^ k) for i in range(n)]))  183 us
    unnamed x9, waiting for transfers between devices  126 us
    pallas_call x1, Pallas kernels, on_device(): pl.pallas_call(functools.partial(attend_kernel, n, shard), grid_spec=pltp...  104 us
    reduce_scatter x1, waiting for transfers between devices, on_device(): up_grad = lax.psum_scatter(up_grad, 'seq', scatter_dimension=0, tiled=True)  69.1 us
    ppermute x21, starting transfers between devices, swap(): out.append(lax.ppermute(parts[k], 'seq', [(i, i ^ k) for i in range(n)]))  47.7 us
    all_gather x1, waiting for transfers between devices, on_device(): lax.all_gather(row_grad, 'mlp', axis=0, tiled=True)  44.9 us
    pallas_call x1, Pallas kernels, on_device(): pl.pallas_call(functools.partial(close_kernel, n, heads, slices), grid_sp...  27.1 us
    reduce_scatter x1, waiting for transfers between devices, on_device(): lax.psum_scatter(low.reshape(rows, width), 'mlp', scatter_dimension=0, ti...  26.7 us
  transfers between devices with their start and end apart: 28, of which 17 were waited for; matrix products, arithmetic and copies ran while one was open for 14% of the time, Pallas kernels for 4%

profile of v1, /device:TPU:17, one launch (start us, length us, event | category | flops | bytes accessed | tf_op | source)
XLA Modules:
  0.0 864.8 jit_solution(12861314882638741687)
XLA Ops:
  10.8 2.6 copy.60
  15.4 2.3 multiply_sine_fusion
  17.7 19.0 %heads.1 = (bf16[12,256,1024]{2,1,0:T(8,128)(2,1)}, bf16[6,3,64,256]{3,2,1,0:T(8,128)(2,1)}, bf16[6,3,64,256]{3,2,1,0:T(8,128)(2,1)}, bf16[6,3,64,256]{3,2,1,0:T...) custom-call(s32[1]{0:T(128)} %bitcast.me_ref, ...), custom_call_target="tpu_custom_call" | custom-call | flops 4831838208 | bytes 17301504 | tf_op jit(solution)/shard_map/heads/pallas_call | solution.py:294
  39.4 3.3 collective-permute-start.4
  42.7 8.8 %fusion.25 = f32[12,256,1024]{2,1,0:T(8,128)S(1)} fusion(bf16[12,256,1024]{2,1,0:T(8,128)(2,1)} %get-tuple-element.62.refs_8_, bf16[1024,1024]{1,0:T(8,128)(2,1)S(1)} %copy-done.5), kind=kOutput, calls=%fused_computation.41 | convolution fusion | flops 6442450944 | bytes 20971520 | tf_op jit(solution)/shard_map/psd,df->psf/dot_general | solution.py:354
  51.6 4.5 copy-done.30
  56.1 10.2 %convolution_convert_fusion.1.refs_14_ = bf16[12,256,1024]{2,1,0:T(8,128)(2,1)} fusion(bf16[1024,1024]{1,0:T(8,128)(2,1)S(1)} %copy-done, f32[12,256,1024]{2,1,0:T(8,128)S(1)} %fusion.25, f32[1024]{0:T(1024)S(1)} %copy-done.28), kind=kOutput, calls=%fused_computation.27 | convolution fusion | flops 6477053952 | bytes 20975616 | tf_op jit(solution)/shard_map/psf,fd->psd/dot_general | solution.py:362
  66.9 7.0 collective-permute-done.1.refs_2_
  75.1 11.6 %out_grads.1 = (bf16[6,64,256]{2,1,0:T(8,128)(2,1)}, bf16[6,64,256]{2,1,0:T(8,128)(2,1)}, bf16[6,64,256]{2,1,0:T(8,128)(2,1)}, bf16[6,64,256]{2,1,0:T(8,128)(2,1...) custom-call(s32[1]{0:T(128)} %bitcast.me_ref, ...), custom_call_target="tpu_custom_call" | custom-call | flops 1610612736 | bytes 7864320 | tf_op jit(solution)/shard_map/out_grads/pallas_call | solution.py:333
  86.7 2.1 collective-permute-start.7
  88.9 3.1 collective-permute-start.8
  92.5 25.9 %collective-permute-start.9 = (bf16[6,64,256]{2,1,0:T(8,128)(2,1)}, bf16[6,64,256]{2,1,0:T(8,128)(2,1)S(1)}, u32[]{:S(2)}, u32[]{:S(2)}) collective-permute-start(bf16[6,64,256]{2,1,0:T(8,128)(2,1)} %get-tuple-element.49), channel_id=1, source_target_pairs={{0,12},{4,8},{8,4},{12,0},{16,28},{20,24},{24,20},{28,16},{1,13},{... | collective-permute-start | bytes 589832 | tf_op jit(solution)/shard_map/ppermute | solution.py:225
  118.3 11.6 %collective-permute-done.5.refs_6_ = bf16[6,3,64,256]{3,2,1,0:T(8,128)(2,1)} collective-permute-done((bf16[6,3,64,256]{3,2,1,0:T(8,128)(2,1)}, bf16[6,3,64,256]{3,2,1,0:T(8,128)(2,1)}, u32[]{:S(2)}, u32[]{:S(2)}) %collective-permute-start.5) | collective-permute-done | bytes 589856 | tf_op jit(solution)/shard_map/ppermute | solution.py:225
  129.9 17.8 %collective-permute-done.6.refs_7_ = bf16[6,3,64,256]{3,2,1,0:T(8,128)(2,1)} collective-permute-done((bf16[6,3,64,256]{3,2,1,0:T(8,128)(2,1)}, bf16[6,3,64,256]{3,2,1,0:T(8,128)(2,1)}, u32[]{:S(2)}, u32[]{:S(2)}) %collective-permute-start.6) | collective-permute-done | bytes 589856 | tf_op jit(solution)/shard_map/ppermute | solution.py:225
  149.9 16.2 %collective-permute-done.11.refs_13_ = bf16[6,64,256]{2,1,0:T(8,128)(2,1)S(1)} collective-permute-done((bf16[6,64,256]{2,1,0:T(8,128)(2,1)}, bf16[6,64,256]{2,1,0:T(8,128)(2,1)S(1)}, u32[]{:S(2)}, u32[]{:S(2)}) %collective-permute-start.11) | collective-permute-done | bytes 196640 | tf_op jit(solution)/shard_map/ppermute | solution.py:225
  166.1 5.8 collective-permute-done.12.refs_14_
  172.0 5.1 collective-permute-done.13.refs_15_
  177.8 104.2 %attend.1 = (bf16[6,4,64,256]{3,2,1,0:T(8,128)(2,1)}, bf16[6,4,64,256]{3,2,1,0:T(8,128)(2,1)}, bf16[6,4,64,256]{3,2,1,0:T(8,128)(2,1)}, bf16[6,4,64,256]{3,2,1,0...) custom-call(s32[1]{0:T(128)} %bitcast.me_ref, ...), custom_call_target="tpu_custom_call" | custom-call | flops 22548578304 | bytes 12582912 | tf_op jit(solution)/shard_map/attend/pallas_call | solution.py:383
  282.4 19.6 %convert_reduce_fusion.1 = (f32[1024]{0:T(1024)S(1)}, bf16[12,256,1024]{2,1,0:T(8,128)(2,1)}) fusion(f32[12,256,1024]{2,1,0:T(8,128)} %copy-done.30, f32[1024]{0:T(1024)S(1)} %copy-done.28, bf16[12,256,1024]{2,1,0:T(8,128)(2,1)} %all-gather.3.cloned.1.call-done.c_ref.refs_9_, bf16[1024,1024]{1,0:T(8,128)(2,1)S(1)} %copy-done), kind=kOutput, calls=%fused_computation.11 | convolution fusion | flops 6514801664 | bytes 27271168 | tf_op jit(solution)/shard_map/psd,fd->psf/dot_general | solution.py:357
  302.1 2.2 collective-permute-start.16
  304.3 2.2 collective-permute-start.17
  307.0 2.5 collective-permute-start.19
  310.1 11.5 %convolution_convert_fusion.refs_15_ = bf16[12,256,1024]{2,1,0:T(8,128)(2,1)} fusion(bf16[12,256,1024]{2,1,0:T(8,128)(2,1)} %get-tuple-element.83, bf16[1024,1024]{1,0:T(8,128)(2,1)S(1)} %copy-done.6), kind=kOutput, calls=%fused_computation.26 | convolution fusion | flops 6445596672 | bytes 14680064 | tf_op jit(solution)/shard_map/psf,df->psd/dot_general | solution.py:365
  321.5 14.7 %collective-permute-done.16.refs_3_ = bf16[6,4,64,256]{3,2,1,0:T(8,128)(2,1)S(1)} collective-permute-done((bf16[6,4,64,256]{3,2,1,0:T(8,128)(2,1)S(1)}, bf16[6,4,64,256]{3,2,1,0:T(8,128)(2,1)S(1)}, u32[]{:S(2)}, u32[]{:S(2)}) %collective-permute-start.16) | collective-permute-done | bytes 786464 | tf_op jit(solution)/shard_map/ppermute | solution.py:225
  336.3 2.8 collective-permute-done.17.refs_4_
  339.1 66.4 %collective-permute-done.18.refs_5_ = bf16[6,4,64,256]{3,2,1,0:T(8,128)(2,1)S(1)} collective-permute-done((bf16[6,4,64,256]{3,2,1,0:T(8,128)(2,1)S(1)}, bf16[6,4,64,256]{3,2,1,0:T(8,128)(2,1)S(1)}, u32[]{:S(2)}, u32[]{:S(2)}) %collective-permute-start.18) | collective-permute-done | bytes 786464 | tf_op jit(solution)/shard_map/ppermute | solution.py:225
  405.6 17.7 %collective-permute-done.19.refs_6_ = bf16[6,4,64,256]{3,2,1,0:T(8,128)(2,1)S(1)} collective-permute-done((bf16[6,4,64,256]{3,2,1,0:T(8,128)(2,1)S(1)}, bf16[6,4,64,256]{3,2,1,0:T(8,128)(2,1)S(1)}, u32[]{:S(2)}, u32[]{:S(2)}) %collective-permute-start.19) | collective-permute-done | bytes 786464 | tf_op jit(solution)/shard_map/ppermute | solution.py:225
  423.3 17.4 %collective-permute-done.20.refs_7_ = bf16[6,4,64,256]{3,2,1,0:T(8,128)(2,1)S(1)} collective-permute-done((bf16[6,4,64,256]{3,2,1,0:T(8,128)(2,1)S(1)}, bf16[6,4,64,256]{3,2,1,0:T(8,128)(2,1)S(1)}, u32[]{:S(2)}, u32[]{:S(2)}) %collective-permute-start.20) | collective-permute-done | bytes 786464 | tf_op jit(solution)/shard_map/ppermute | solution.py:225
  441.6 27.1 %close.1 = (bf16[4,12,256,256]{3,2,1,0:T(8,128)(2,1)}, bf16[12,256,1024]{2,1,0:T(8,128)(2,1)}, bf16[1024,1024]{1,0:T(8,128)(2,1)}) custom-call(s32[1]{0:T(128)} %bitcast.me_ref, s32[3,6]{1,0:T(4,128)} %concatenate.3.pack_ref, bf16[6,4,64,256]{3,2,1,0:T(8,128)(2,1)} %get-tuple-element.54.refs_0_, bf16[6,4,64,256]{3,2,1,0:T(8,128)(2,1)} %copy-done.11, ...), custom_call_target="tpu_custom_call" | custom-call | flops 12884901888 | bytes 44040192 | tf_op jit(solution)/shard_map/close/pallas_call | solution.py:408
  468.8 12.0 %fusion.27 = bf16[1024,1024]{0,1:T(8,128)(2,1)S(1)} fusion(bf16[12,256,1024]{2,1,0:T(8,128)(2,1)} %all-gather.3.cloned.1.call-done.c_ref.refs_9_, f32[12,256,1024]{2,1,0:T(8,128)} %copy-done.30, f32[1024]{0:T(1024)S(1)} %copy-done.28), kind=kOutput, calls=%fused_computation.43 | convolution fusion | flops 6474956800 | bytes 20975616 | tf_op jit(solution)/shard_map/psd,psf->df/dot_general | solution.py:371
  480.8 2.7 copy.72
  483.6 12.2 %bitcast_convert_fusion.1 = bf16[1024,1024]{1,0:T(8,128)(2,1)} fusion(bf16[12,256,1024]{2,1,0:T(8,128)(2,1)} %get-tuple-element.62.refs_8_, bf16[12,256,1024]{2,1,0:T(8,128)(2,1)} %get-tuple-element.83), kind=kOutput, calls=%fused_computation.20 | convolution fusion | flops 6443499520 | bytes 14680064 | tf_op jit(solution)/shard_map/psd,psf->df/dot_general | solution.py:368
  495.8 2.6 copy.70
  500.7 2.0 fusion.17
  502.7 26.7 %reduce-scatter.12.cloned.1.call-done = bf16[768,1024]{1,0:T(8,128)(2,1)} async-done(((bf16[3072,1024]{1,0:T(8,128)(2,1)}), bf16[768,1024]{1,0:T(8,128)(2,1)}) %reduce-scatter.12.cloned.1.call-update) | async-done | bytes 1572880 | tf_op jit(solution)/shard_map/reduce_scatter | solution.py:472
  529.4 3.3 fusion.19
  532.7 4.2 fusion.16
  539.0 3.9 convert_reduce_fusion
  542.9 55.9 %reduce-scatter.18.cloned.1.call-done = bf16[128,1024]{1,0:T(8,128)(2,1)} async-done(((bf16[1024,1024]{1,0:T(8,128)(2,1)}), bf16[128,1024]{1,0:T(8,128)(2,1)}) %reduce-scatter.18.cloned.1.call-update) | async-done | bytes 262160
  599.9 69.1 %reduce-scatter.14.cloned.1.call-done = bf16[128,1024]{1,0:T(8,128)(2,1)} async-done(((bf16[1024,1024]{1,0:T(8,128)(2,1)}), bf16[128,1024]{1,0:T(8,128)(2,1)}) %reduce-scatter.14.cloned.1.call-update) | async-done | bytes 262160 | tf_op jit(solution)/shard_map/reduce_scatter | solution.py:372
  669.0 1.8 convert_element_type.80
  671.6 68.7 %reduce-scatter.16.cloned.1.call-done = bf16[128,1024]{1,0:T(8,128)(2,1)} async-done(((bf16[1024,1024]{1,0:T(8,128)(2,1)}), bf16[128,1024]{1,0:T(8,128)(2,1)}) %reduce-scatter.16.cloned.1.call-update) | async-done | bytes 262160
  744.0 24.1 %all-reduce.5 = (f32[1024]{0:T(1024)S(1)}, f32[1024]{0:T(1024)S(1)}, f32[1024]{0:T(1024)S(1)}, f32[1024]{0:T(1024)S(1)}) all-reduce(f32[1024]{0:T(1024)S(1)} %get-tuple-element.66, f32[1024]{0:T(1024)S(1)} %get-tuple-element.69, f32[1024]{0:T(1024)S(1)} %get-tuple-element.82, ...), channel_id=4, replica_groups=mesh['seq'=8,'mlp'=4] {'seq'}, use_global_device_ids=true, to_apply=%region_14.15.clone | all-reduce | flops 4096 | bytes 32768
  769.4 13.9 %all-reduce.6 = (f32[128]{0:T(128)}, f32[128]{0:T(128)}) all-reduce(f32[128]{0:T(128)S(1)} %dynamic-slice.1, f32[128]{0:T(128)S(1)} %dynamic-slice.3), channel_id=1, replica_groups=mesh['seq'=8,'mlp'=4] {'mlp'}, use_global_device_ids=true, to_apply=%region_13.14 | all-reduce | flops 256 | bytes 2048 | tf_op jit(solution)/shard_map/psum | solution.py:495
  783.3 19.5 %reduce-scatter.10.cloned.1.call-done = bf16[1,12,256,256]{3,2,1,0:T(8,128)(2,1)} async-done(((bf16[4,12,256,256]{3,2,1,0:T(8,128)(2,1)}), bf16[1,12,256,256]{3,2,1,0:T(8,128)(2,1)}) %reduce-scatter.10.cloned.1.call-update) | async-done | bytes 1572880 | tf_op jit(solution)/shard_map/reduce_scatter | solution.py:463
  802.8 3.5 fusion.21
  806.3 44.9 %all-gather.5.cloned.1.call-done = bf16[3072,1024]{1,0:T(8,128)(2,1)} async-done(((bf16[768,1024]{1,0:T(8,128)(2,1)}), bf16[3072,1024]{1,0:T(8,128)(2,1)}) %all-gather.5.cloned.1.call-update) | async-done | bytes 6291472 | tf_op jit(solution)/shard_map/all_gather | solution.py:494
  851.2 6.3 copy.79
  (150 shorter events, 26.5 us)
Async XLA Ops:
  7.2 48.9 %copy-start = (bf16[1024,1024]{1,0:T(8,128)(2,1)S(1)}, bf16[1024,1024]{1,0:T(8,128)(2,1)}, u32[]{:S(2)}) copy-start(bf16[1024,1024]{1,0:T(8,128)(2,1)} %param.21) | copy-start | bytes 6291460
  7.2 67.9 %all-gather.3.cloned.1.call-start = ((), (), s32[]{:S(2)}) async-start(), calls=%async_computation.5 | async-start | bytes 7864320 | tf_op jit(solution)/shard_map/all_gather | solution.py:256
  7.9 521.5 %reduce-scatter.12.cloned.1.call-start = ((), (), s32[]{:S(2)}) async-start(), calls=%async_computation.7 | async-start | bytes 7864320 | tf_op jit(solution)/shard_map/reduce_scatter | solution.py:472
  17.7 25.0 %copy-start.5 = (bf16[1024,1024]{1,0:T(8,128)(2,1)S(1)}, bf16[1024,1024]{1,0:T(8,128)(2,1)}, u32[]{:S(2)}) copy-start(bf16[1024,1024]{1,0:T(8,128)(2,1)} %param.19) | copy-start | bytes 6291460
  36.7 29.9 %collective-permute-start = (bf16[6,3,64,256]{3,2,1,0:T(8,128)(2,1)}, bf16[6,3,64,256]{3,2,1,0:T(8,128)(2,1)S(1)}, u32[]{:S(2)}, u32[]{:S(2)}) collective-permute-start(bf16[6,3,64,256]{3,2,1,0:T(8,128)(2,1)} %get-tuple-element.39), channel_id=1, source_target_pairs={{0,4},{4,0},{8,12},{12,8},{16,20},{20,16},{24,28},{28,24},{1,5},{5... | collective-permute-start | bytes 1769480 | tf_op jit(solution)/shard_map/ppermute | solution.py:225
  38.0 36.0 %collective-permute-start.1 = (bf16[6,3,64,256]{3,2,1,0:T(8,128)(2,1)}, bf16[6,3,64,256]{3,2,1,0:T(8,128)(2,1)S(1)}, u32[]{:S(2)}, u32[]{:S(2)}) collective-permute-start(bf16[6,3,64,256]{3,2,1,0:T(8,128)(2,1)} %get-tuple-element.40), channel_id=1, source_target_pairs={{0,8},{4,12},{8,0},{12,4},{16,24},{20,28},{24,16},{28,20},{1,9},{5... | collective-permute-start | bytes 1769480 | tf_op jit(solution)/shard_map/ppermute | solution.py:225
  39.3 47.5 %collective-permute-start.2 = (bf16[6,3,64,256]{3,2,1,0:T(8,128)(2,1)}, bf16[6,3,64,256]{3,2,1,0:T(8,128)(2,1)}, u32[]{:S(2)}, u32[]{:S(2)}) collective-permute-start(bf16[6,3,64,256]{3,2,1,0:T(8,128)(2,1)} %get-tuple-element.41), channel_id=1, source_target_pairs={{0,12},{4,8},{8,4},{12,0},{16,28},{20,24},{24,20},{28,16},{1,13},{... | collective-permute-start | bytes 1769480 | tf_op jit(solution)/shard_map/ppermute | solution.py:225
  39.4 49.4 %collective-permute-start.3 = (bf16[6,3,64,256]{3,2,1,0:T(8,128)(2,1)}, bf16[6,3,64,256]{3,2,1,0:T(8,128)(2,1)}, u32[]{:S(2)}, u32[]{:S(2)}) collective-permute-start(bf16[6,3,64,256]{3,2,1,0:T(8,128)(2,1)} %get-tuple-element.42), channel_id=1, source_target_pairs={{0,16},{4,20},{8,24},{12,28},{16,0},{20,4},{24,8},{28,12},{1,17},{... | collective-permute-start | bytes 1769480 | tf_op jit(solution)/shard_map/ppermute | solution.py:225
  39.4 53.1 %collective-permute-start.4 = (bf16[6,3,64,256]{3,2,1,0:T(8,128)(2,1)}, bf16[6,3,64,256]{3,2,1,0:T(8,128)(2,1)}, u32[]{:S(2)}, u32[]{:S(2)}) collective-permute-start(bf16[6,3,64,256]{3,2,1,0:T(8,128)(2,1)} %get-tuple-element.43), channel_id=1, source_target_pairs={{0,20},{4,16},{8,28},{12,24},{16,4},{20,0},{24,12},{28,8},{1,21},{... | collective-permute-start | bytes 1769480 | tf_op jit(solution)/shard_map/ppermute | solution.py:225
  66.4 110.7 %copy-start.3 = (s32[12,8,256]{2,1,0:T(8,128)}, s32[12,8,256]{2,1,0:T(8,128)S(1)}, u32[]{:S(2)}) copy-start(s32[12,8,256]{2,1,0:T(8,128)S(1)} %slice_select_fusion.first_ref) | copy-start | bytes 294916
  66.7 110.5 %copy-start.19 = (bf16[6,3,64,256]{3,2,1,0:T(8,128)(2,1)}, bf16[6,3,64,256]{3,2,1,0:T(8,128)(2,1)S(1)}, u32[]{:S(2)}) copy-start(bf16[6,3,64,256]{3,2,1,0:T(8,128)(2,1)S(1)} %collective-permute-done.refs_1_) | copy-start | bytes 1769476
  66.7 63.3 %collective-permute-start.5 = (bf16[6,3,64,256]{3,2,1,0:T(8,128)(2,1)}, bf16[6,3,64,256]{3,2,1,0:T(8,128)(2,1)}, u32[]{:S(2)}, u32[]{:S(2)}) collective-permute-start(bf16[6,3,64,256]{3,2,1,0:T(8,128)(2,1)} %get-tuple-element.44), channel_id=1, source_target_pairs={{0,24},{4,28},{8,16},{12,20},{16,8},{20,12},{24,0},{28,4},{1,25},{... | collective-permute-start | bytes 1769480 | tf_op jit(solution)/shard_map/ppermute | solution.py:225
  73.9 103.2 %copy-start.20 = (bf16[6,3,64,256]{3,2,1,0:T(8,128)(2,1)}, bf16[6,3,64,256]{3,2,1,0:T(8,128)(2,1)S(1)}, u32[]{:S(2)}) copy-start(bf16[6,3,64,256]{3,2,1,0:T(8,128)(2,1)S(1)} %collective-permute-done.1.refs_2_) | copy-start | bytes 1769476
  73.9 73.8 %collective-permute-start.6 = (bf16[6,3,64,256]{3,2,1,0:T(8,128)(2,1)}, bf16[6,3,64,256]{3,2,1,0:T(8,128)(2,1)}, u32[]{:S(2)}, u32[]{:S(2)}) collective-permute-start(bf16[6,3,64,256]{3,2,1,0:T(8,128)(2,1)} %get-tuple-element.45), channel_id=1, source_target_pairs={{0,28},{4,24},{8,20},{12,16},{16,12},{20,8},{24,4},{28,0},{1,29},{... | collective-permute-start | bytes 1769480 | tf_op jit(solution)/shard_map/ppermute | solution.py:225
  86.7 61.0 %collective-permute-start.7 = (bf16[6,64,256]{2,1,0:T(8,128)(2,1)}, bf16[6,64,256]{2,1,0:T(8,128)(2,1)S(1)}, u32[]{:S(2)}, u32[]{:S(2)}) collective-permute-start(bf16[6,64,256]{2,1,0:T(8,128)(2,1)} %get-tuple-element.47), channel_id=1, source_target_pairs={{0,4},{4,0},{8,12},{12,8},{16,20},{20,16},{24,28},{28,24},{1,5},{5... | collective-permute-start | bytes 589832 | tf_op jit(solution)/shard_map/ppermute | solution.py:225
  88.9 59.0 %collective-permute-start.8 = (bf16[6,64,256]{2,1,0:T(8,128)(2,1)}, bf16[6,64,256]{2,1,0:T(8,128)(2,1)S(1)}, u32[]{:S(2)}, u32[]{:S(2)}) collective-permute-start(bf16[6,64,256]{2,1,0:T(8,128)(2,1)} %get-tuple-element.48), channel_id=1, source_target_pairs={{0,8},{4,12},{8,0},{12,4},{16,24},{20,28},{24,16},{28,20},{1,9},{5... | collective-permute-start | bytes 589832 | tf_op jit(solution)/shard_map/ppermute | solution.py:225
  92.5 57.4 %collective-permute-start.9 = (bf16[6,64,256]{2,1,0:T(8,128)(2,1)}, bf16[6,64,256]{2,1,0:T(8,128)(2,1)S(1)}, u32[]{:S(2)}, u32[]{:S(2)}) collective-permute-start(bf16[6,64,256]{2,1,0:T(8,128)(2,1)} %get-tuple-element.49), channel_id=1, source_target_pairs={{0,12},{4,8},{8,4},{12,0},{16,28},{20,24},{24,20},{28,16},{1,13},{... | collective-permute-start | bytes 589832 | tf_op jit(solution)/shard_map/ppermute | solution.py:225
  129.9 20.0 %collective-permute-start.10 = (bf16[6,64,256]{2,1,0:T(8,128)(2,1)}, bf16[6,64,256]{2,1,0:T(8,128)(2,1)S(1)}, u32[]{:S(2)}, u32[]{:S(2)}) collective-permute-start(bf16[6,64,256]{2,1,0:T(8,128)(2,1)} %get-tuple-element.50), channel_id=1, source_target_pairs={{0,16},{4,20},{8,24},{12,28},{16,0},{20,4},{24,8},{28,12},{1,17},{... | collective-permute-start | bytes 589832 | tf_op jit(solution)/shard_map/ppermute | solution.py:225
  147.7 18.4 %collective-permute-start.11 = (bf16[6,64,256]{2,1,0:T(8,128)(2,1)}, bf16[6,64,256]{2,1,0:T(8,128)(2,1)S(1)}, u32[]{:S(2)}, u32[]{:S(2)}) collective-permute-start(bf16[6,64,256]{2,1,0:T(8,128)(2,1)} %get-tuple-element.51), channel_id=1, source_target_pairs={{0,20},{4,16},{8,28},{12,24},{16,4},{20,0},{24,12},{28,8},{1,21},{... | collective-permute-start | bytes 589832 | tf_op jit(solution)/shard_map/ppermute | solution.py:225
  147.7 29.4 %copy-start.21 = (bf16[6,64,256]{2,1,0:T(8,128)(2,1)}, bf16[6,64,256]{2,1,0:T(8,128)(2,1)S(1)}, u32[]{:S(2)}) copy-start(bf16[6,64,256]{2,1,0:T(8,128)(2,1)S(1)} %collective-permute-done.7.refs_9_) | copy-start | bytes 589828
  147.7 24.2 %collective-permute-start.12 = (bf16[6,64,256]{2,1,0:T(8,128)(2,1)}, bf16[6,64,256]{2,1,0:T(8,128)(2,1)S(1)}, u32[]{:S(2)}, u32[]{:S(2)}) collective-permute-start(bf16[6,64,256]{2,1,0:T(8,128)(2,1)} %get-tuple-element.52), channel_id=1, source_target_pairs={{0,24},{4,28},{8,16},{12,20},{16,8},{20,12},{24,0},{28,4},{1,25},{... | collective-permute-start | bytes 589832 | tf_op jit(solution)/shard_map/ppermute | solution.py:225
  147.8 29.3 %copy-start.22 = (bf16[6,64,256]{2,1,0:T(8,128)(2,1)}, bf16[6,64,256]{2,1,0:T(8,128)(2,1)S(1)}, u32[]{:S(2)}) copy-start(bf16[6,64,256]{2,1,0:T(8,128)(2,1)S(1)} %collective-permute-done.8.refs_10_) | copy-start | bytes 589828
  147.8 29.3 %collective-permute-start.13 = (bf16[6,64,256]{2,1,0:T(8,128)(2,1)}, bf16[6,64,256]{2,1,0:T(8,128)(2,1)S(1)}, u32[]{:S(2)}, u32[]{:S(2)}) collective-permute-start(bf16[6,64,256]{2,1,0:T(8,128)(2,1)} %get-tuple-element.53), channel_id=1, source_target_pairs={{0,28},{4,24},{8,20},{12,16},{16,12},{20,8},{24,4},{28,0},{1,29},{... | collective-permute-start | bytes 589832 | tf_op jit(solution)/shard_map/ppermute | solution.py:225
  149.9 27.2 %copy-start.23 = (bf16[6,64,256]{2,1,0:T(8,128)(2,1)}, bf16[6,64,256]{2,1,0:T(8,128)(2,1)S(1)}, u32[]{:S(2)}) copy-start(bf16[6,64,256]{2,1,0:T(8,128)(2,1)S(1)} %collective-permute-done.9.refs_11_) | copy-start | bytes 589828
  149.9 27.3 %copy-start.24 = (bf16[6,64,256]{2,1,0:T(8,128)(2,1)}, bf16[6,64,256]{2,1,0:T(8,128)(2,1)S(1)}, u32[]{:S(2)}) copy-start(bf16[6,64,256]{2,1,0:T(8,128)(2,1)S(1)} %collective-permute-done.10.refs_12_) | copy-start | bytes 589828
  282.0 25.0 %collective-permute-start.14 = (bf16[6,4,64,256]{3,2,1,0:T(8,128)(2,1)}, bf16[6,4,64,256]{3,2,1,0:T(8,128)(2,1)S(1)}, u32[]{:S(2)}, u32[]{:S(2)}) collective-permute-start(bf16[6,4,64,256]{3,2,1,0:T(8,128)(2,1)} %get-tuple-element.55), channel_id=1, source_target_pairs={{0,4},{4,0},{8,12},{12,8},{16,20},{20,16},{24,28},{28,24},{1,5},{5... | collective-permute-start | bytes 2359304 | tf_op jit(solution)/shard_map/ppermute | solution.py:225
  282.3 19.7 %copy-start.12 = (bf16[6,4,64,256]{3,2,1,0:T(8,128)(2,1)S(1)}, bf16[6,4,64,256]{3,2,1,0:T(8,128)(2,1)}, u32[]{:S(2)}) copy-start(bf16[6,4,64,256]{3,2,1,0:T(8,128)(2,1)} %get-tuple-element.57) | copy-start | bytes 2359300
  282.3 22.0 %copy-start.10 = (bf16[6,4,64,256]{3,2,1,0:T(8,128)(2,1)S(1)}, bf16[6,4,64,256]{3,2,1,0:T(8,128)(2,1)}, u32[]{:S(2)}) copy-start(bf16[6,4,64,256]{3,2,1,0:T(8,128)(2,1)} %get-tuple-element.58) | copy-start | bytes 2359300
  282.3 24.1 %copy-start.9 = (bf16[6,4,64,256]{3,2,1,0:T(8,128)(2,1)S(1)}, bf16[6,4,64,256]{3,2,1,0:T(8,128)(2,1)}, u32[]{:S(2)}) copy-start(bf16[6,4,64,256]{3,2,1,0:T(8,128)(2,1)} %get-tuple-element.59) | copy-start | bytes 2359300
  282.3 24.7 %copy-start.8 = (bf16[6,4,64,256]{3,2,1,0:T(8,128)(2,1)S(1)}, bf16[6,4,64,256]{3,2,1,0:T(8,128)(2,1)}, u32[]{:S(2)}) copy-start(bf16[6,4,64,256]{3,2,1,0:T(8,128)(2,1)} %get-tuple-element.60) | copy-start | bytes 2359300
  282.3 27.2 %copy-start.7 = (bf16[6,4,64,256]{3,2,1,0:T(8,128)(2,1)S(1)}, bf16[6,4,64,256]{3,2,1,0:T(8,128)(2,1)}, u32[]{:S(2)}) copy-start(bf16[6,4,64,256]{3,2,1,0:T(8,128)(2,1)} %get-tuple-element.61) | copy-start | bytes 2359300
  282.4 27.7 %copy-start.6 = (bf16[1024,1024]{1,0:T(8,128)(2,1)S(1)}, bf16[1024,1024]{1,0:T(8,128)(2,1)}, u32[]{:S(2)}) copy-start(bf16[1024,1024]{1,0:T(8,128)(2,1)} %param.19) | copy-start | bytes 6291460
  282.4 27.1 %collective-permute-start.15 = (bf16[6,4,64,256]{3,2,1,0:T(8,128)(2,1)}, bf16[6,4,64,256]{3,2,1,0:T(8,128)(2,1)S(1)}, u32[]{:S(2)}, u32[]{:S(2)}) collective-permute-start(bf16[6,4,64,256]{3,2,1,0:T(8,128)(2,1)} %get-tuple-element.56), channel_id=1, source_target_pairs={{0,8},{4,12},{8,0},{12,4},{16,24},{20,28},{24,16},{28,20},{1,9},{5... | collective-permute-start | bytes 2359304 | tf_op jit(solution)/shard_map/ppermute | solution.py:225
  302.1 34.2 %collective-permute-start.16 = (bf16[6,4,64,256]{3,2,1,0:T(8,128)(2,1)S(1)}, bf16[6,4,64,256]{3,2,1,0:T(8,128)(2,1)S(1)}, u32[]{:S(2)}, u32[]{:S(2)}) collective-permute-start(bf16[6,4,64,256]{3,2,1,0:T(8,128)(2,1)S(1)} %copy-done.12), channel_id=1, source_target_pairs={{0,12},{4,8},{8,4},{12,0},{16,28},{20,24},{24,20},{28,16},{1,13},{... | collective-permute-start | bytes 2359304 | tf_op jit(solution)/shard_map/ppermute | solution.py:225
  304.3 34.8 %collective-permute-start.17 = (bf16[6,4,64,256]{3,2,1,0:T(8,128)(2,1)S(1)}, bf16[6,4,64,256]{3,2,1,0:T(8,128)(2,1)S(1)}, u32[]{:S(2)}, u32[]{:S(2)}) collective-permute-start(bf16[6,4,64,256]{3,2,1,0:T(8,128)(2,1)S(1)} %copy-done.10), channel_id=1, source_target_pairs={{0,16},{4,20},{8,24},{12,28},{16,0},{20,4},{24,8},{28,12},{1,17},{... | collective-permute-start | bytes 2359304 | tf_op jit(solution)/shard_map/ppermute | solution.py:225
  306.5 99.1 %collective-permute-start.18 = (bf16[6,4,64,256]{3,2,1,0:T(8,128)(2,1)S(1)}, bf16[6,4,64,256]{3,2,1,0:T(8,128)(2,1)S(1)}, u32[]{:S(2)}, u32[]{:S(2)}) collective-permute-start(bf16[6,4,64,256]{3,2,1,0:T(8,128)(2,1)S(1)} %copy-done.9), channel_id=1, source_target_pairs={{0,20},{4,16},{8,28},{12,24},{16,4},{20,0},{24,12},{28,8},{1,21},{... | collective-permute-start | bytes 2359304 | tf_op jit(solution)/shard_map/ppermute | solution.py:225
  307.0 116.2 %collective-permute-start.19 = (bf16[6,4,64,256]{3,2,1,0:T(8,128)(2,1)S(1)}, bf16[6,4,64,256]{3,2,1,0:T(8,128)(2,1)S(1)}, u32[]{:S(2)}, u32[]{:S(2)}) collective-permute-start(bf16[6,4,64,256]{3,2,1,0:T(8,128)(2,1)S(1)} %copy-done.8), channel_id=1, source_target_pairs={{0,24},{4,28},{8,16},{12,20},{16,8},{20,12},{24,0},{28,4},{1,25},{... | collective-permute-start | bytes 2359304 | tf_op jit(solution)/shard_map/ppermute | solution.py:225
  309.5 131.2 %collective-permute-start.20 = (bf16[6,4,64,256]{3,2,1,0:T(8,128)(2,1)S(1)}, bf16[6,4,64,256]{3,2,1,0:T(8,128)(2,1)S(1)}, u32[]{:S(2)}, u32[]{:S(2)}) collective-permute-start(bf16[6,4,64,256]{3,2,1,0:T(8,128)(2,1)S(1)} %copy-done.7), channel_id=1, source_target_pairs={{0,28},{4,24},{8,20},{12,16},{16,12},{20,8},{24,4},{28,0},{1,29},{... | collective-permute-start | bytes 2359304 | tf_op jit(solution)/shard_map/ppermute | solution.py:225
  336.3 104.4 %copy-start.14 = (bf16[6,4,64,256]{3,2,1,0:T(8,128)(2,1)}, bf16[6,4,64,256]{3,2,1,0:T(8,128)(2,1)S(1)}, u32[]{:S(2)}) copy-start(bf16[6,4,64,256]{3,2,1,0:T(8,128)(2,1)S(1)} %collective-permute-done.16.refs_3_) | copy-start | bytes 2359300
  339.1 101.6 %copy-start.15 = (bf16[6,4,64,256]{3,2,1,0:T(8,128)(2,1)}, bf16[6,4,64,256]{3,2,1,0:T(8,128)(2,1)S(1)}, u32[]{:S(2)}) copy-start(bf16[6,4,64,256]{3,2,1,0:T(8,128)(2,1)S(1)} %collective-permute-done.17.refs_4_) | copy-start | bytes 2359300
  405.6 35.2 %copy-start.16 = (bf16[6,4,64,256]{3,2,1,0:T(8,128)(2,1)}, bf16[6,4,64,256]{3,2,1,0:T(8,128)(2,1)S(1)}, u32[]{:S(2)}) copy-start(bf16[6,4,64,256]{3,2,1,0:T(8,128)(2,1)S(1)} %collective-permute-done.18.refs_5_) | copy-start | bytes 2359300
  468.7 130.1 %reduce-scatter.18.cloned.1.call-start = ((), (), s32[]{:S(2)}) async-start(), calls=%async_computation.11 | async-start | bytes 2359296
  483.5 185.5 %reduce-scatter.14.cloned.1.call-start = ((), (), s32[]{:S(2)}) async-start(), calls=%async_computation.9 | async-start | bytes 2359296 | tf_op jit(solution)/shard_map/reduce_scatter | solution.py:372
  495.7 244.6 %reduce-scatter.16.cloned.1.call-start = ((), (), s32[]{:S(2)}) async-start(), calls=%async_computation.10 | async-start | bytes 2359296
  498.4 31.0 %copy-start.4 = (f32[1024]{0:T(1024)S(1)}, f32[1024]{0:T(1024)}, u32[]{:S(2)}) copy-start(f32[1024]{0:T(1024)} %param.15) | copy-start | bytes 12292
  498.4 304.4 %reduce-scatter.10.cloned.1.call-start = ((), (), s32[]{:S(2)}) async-start(), calls=%async_computation.6 | async-start | bytes 7864320 | tf_op jit(solution)/shard_map/reduce_scatter | solution.py:463
  499.0 352.2 %all-gather.5.cloned.1.call-start = ((), (), s32[]{:S(2)}) async-start(), calls=%async_computation.8 | async-start | bytes 7864320 | tf_op jit(solution)/shard_map/all_gather | solution.py:494
  500.7 36.3 %copy-start.29 = (u32[32]{0:T(128)S(1)}, u32[32]{0:T(128)}, u32[]{:S(2)}) copy-start(u32[32]{0:T(128)} %constant.129) | copy-start | bytes 388
  (11 other events, 98.4 us)
Sparse Core Ops, SparseCore 0:
  9.6 48.7 all-gather.2
  468.8 60.5 reduce-scatter.11
  533.4 65.4 reduce-scatter.17
  602.6 66.3 reduce-scatter.13
  673.4 66.9 reduce-scatter.15
  742.9 59.8 reduce-scatter.9
  804.4 46.7 all-gather.4

commit v2 on v1

--- a/solution.py
+++ b/solution.py
@@ -96,46 +96,64 @@
             outs[k][0] = scr[d % heads]
 
 
-def attend_kernel(n, block, me_ref, pack_ref, low_ref, first_ref, *refs):
-    qkv, grads, outs = refs[:n], refs[n : 2 * n], refs[2 * n : 3 * n]
-    qt, kt, vt, gt, qn, kn, vn, gn, dk, dv, res = refs[3 * n :]
-    s_id = pl.program_id(0)
-    me = me_ref[0]
+def load_parts(n, me, pairs):
     for k in range(n):
         d = lax.bitwise_xor(jnp.int32(k), me)
-        for j, (t_ref, n_ref) in enumerate(((qt, qn), (kt, kn), (vt, vn), (gt, gn))):
-            part = qkv[k][0, j] if j < 3 else grads[k][0]
-            t_ref[d] = part
-            n_ref[d] = part.T
-    dk[...] = jnp.zeros_like(dk)
-    dv[...] = jnp.zeros_like(dv)
+        for part, t_ref, n_ref in pairs(k):
+            if t_ref is not None:
+                t_ref[d] = part
+            if n_ref is not None:
+                n_ref[d] = part.T
+
+
+def score_of(block, first, i, kn, q_t):
     rows = lax.broadcasted_iota(jnp.int32, (block, block), 0)
     cols = lax.broadcasted_iota(jnp.int32, (block, block), 1)
     ahead = rows - cols
 
+    def scores(j, at):
+        s = dot(kn[at], q_t)
+        allowed = (rows >= first - j * block) & (ahead <= (i - j) * block)
+        return jnp.where(allowed, s, NEG)
+
+    return scores
+
+
+def attend_kernel(n, block, me_ref, pack_ref, low_ref, first_ref, *refs):
+    qkv, outs, keep_ref, logsum_ref = refs[:n], refs[n : 2 * n], refs[2 * n], refs[2 * n + 1]
+    qt, vt, kn = refs[2 * n + 2 :]
+    s_id = pl.program_id(0)
+    me = me_ref[0]
+    load_parts(
+        n,
+        me,
+        lambda k: (
+            (qkv[k][0, 0], qt, None),
+            (qkv[k][0, 1], None, kn),
+            (qkv[k][0, 2], vt, None),
+        ),
+    )
+
     def outer(i, carry):
-        q_t, g_t, q_n, g_n = qt[i], gt[i], qn[i], gn[i]
-        first = first_ref[0, pl.ds(i, 1), :]
+        scores = score_of(block, first_ref[0, pl.ds(i, 1), :], i, kn, qt[i])
         j0 = low_ref[s_id, i]
 
-        def scores(j):
-            s = dot(kn[j], q_t)
-            allowed = (rows >= first - j * block) & (ahead <= (i - j) * block)
-            return jnp.where(allowed, s, NEG)
-
-        def forward(j, state):
+        def forward(t, state):
             top, total, acc = state
-            s = scores(j)
-            new_top = jnp.maximum(top, jnp.max(s, axis=0, keepdims=True))
-            p = jnp.exp(s - new_top)
+            j = j0 + 2 * t
+            at = jnp.minimum(j + 1, n - 1)
+            s0, s1 = scores(j, j), scores(j + 1, at)
+            peak = jnp.max(jnp.maximum(s0, s1), axis=0, keepdims=True)
+            new_top = jnp.maximum(top, peak)
+            p0, p1 = jnp.exp(s0 - new_top), jnp.exp(s1 - new_top)
             fade = jnp.exp(top - new_top)
-            total = total * fade + jnp.sum(p, axis=0, keepdims=True)
-            acc = acc * fade + dot(vt[j], p.astype(BF16))
+            total = total * fade + jnp.sum(p0 + p1, axis=0, keepdims=True)
+            acc = acc * fade + dot(vt[j], p0.astype(BF16)) + dot(vt[at], p1.astype(BF16))
             return new_top, total, acc
 
         top, total, acc = lax.fori_loop(
-            j0,
-            i + 1,
+            0,
+            (i - j0) // 2 + 1,
             forward,
             (
                 jnp.full((1, block), NEG, F32),
@@ -143,36 +161,105 @@
                 jnp.zeros((HD, block), F32),
             ),
         )
-        acc = acc / total
-        logsum = top + jnp.log(total)
-        inner = jnp.sum(acc * g_t.astype(F32), axis=0, keepdims=True)
-        res[i, 0] = acc.astype(BF16)
-
-        def backward(j, dq):
-            p = jnp.exp(scores(j) - logsum)
-            dp = dot(vn[j], g_t)
-            ds = (p * (dp - inner)).astype(BF16)
-            dk[j] += dot(ds, q_n)
-            dv[j] += dot(p.astype(BF16), g_n)
-            return dq + dot(kt[j], ds)
-
-        dq = lax.fori_loop(j0, i + 1, backward, jnp.zeros((HD, block), F32))
-        res[i, 1] = (dq * (1.0 / math.sqrt(HD))).astype(BF16)
+        keep_ref[0, i] = (acc / total).astype(BF16)
+        logsum_ref[0, pl.ds(i, 1), :] = top + jnp.log(total)
+        return carry
+
+    lax.fori_loop(0, n, outer, 0)
+    for k in range(n):
+        outs[k][0] = keep_ref[0, lax.bitwise_xor(jnp.int32(k), me)]
+
+
+def attend_back_kernel(n, block, me_ref, pack_ref, low_ref, first_ref, *refs):
+    keep_ref, logsum_ref = refs[:2]
+    qkv, grads, outs = refs[2 : n + 2], refs[n + 2 : 2 * n + 2], refs[2 * n + 2 : 3 * n + 2]
+    qt, kt, gt, qn, kn, vn, gn, dk, dv, res = refs[3 * n + 2 :]
+    s_id = pl.program_id(0)
+    me = me_ref[0]
+    load_parts(
+        n,
+        me,
+        lambda k: (
+            (qkv[k][0, 0], qt, qn),
+            (qkv[k][0, 1], kt, kn),
+            (qkv[k][0, 2], None, vn),
+            (grads[k][0], gt, gn),
+        ),
+    )
+    dk[...] = jnp.zeros_like(dk)
+    dv[...] = jnp.zeros_like(dv)
+
+    def outer(i, carry):
+        q_t, g_t, q_n, g_n = qt[i], gt[i], qn[i], gn[i]
+        scores = score_of(block, first_ref[0, pl.ds(i, 1), :], i, kn, q_t)
+        j0 = low_ref[s_id, i]
+        inner = jnp.sum(keep_ref[0, i].astype(F32) * g_t.astype(F32), axis=0, keepdims=True)
+        logsum = logsum_ref[0, pl.ds(i, 1), :]
+
+        def one(j, at):
+            p = jnp.exp(scores(j, at) - logsum)
+            ds = (p * (dot(vn[at], g_t) - inner)).astype(BF16)
+            return ds, dot(ds, q_n), dot(p.astype(BF16), g_n), dot(kt[at], ds)
+
+        def backward(t, dq):
+            j = j0 + 2 * t
+            at = jnp.minimum(j + 1, n - 1)
+            _, dk0, dv0, dq0 = one(j, j)
+            _, dk1, dv1, dq1 = one(j + 1, at)
+            dk[j] += dk0
+            dv[j] += dv0
+            dk[at] += dk1
+            dv[at] += dv1
+            return dq + dq0 + dq1
+
+        dq = lax.fori_loop(0, (i - j0) // 2 + 1, backward, jnp.zeros((HD, block), F32))
+        res[i, 0] = (dq * (1.0 / math.sqrt(HD))).astype(BF16)
         return carry
 
     lax.fori_loop(0, n, outer, 0)
     for i in range(n):
-        res[i, 2] = dk[i].T.astype(BF16)
-        res[i, 3] = dv[i].T.astype(BF16)
+        res[i, 1] = dk[i].T.astype(BF16)
+        res[i, 2] = dv[i].T.astype(BF16)
+    for k in range(n):
+        outs[k][0] = res[lax.bitwise_xor(jnp.int32(k), me)]
+
+
+def merge_kernel(n, heads, slices, me_ref, pack_ref, *refs):
+    recv = refs[:n]
+    c_ref, merge_ref, branch_ref, out_branch, out_weight, scr, acc = refs[n:]
+    s_id, g = pl.program_id(0), pl.program_id(1)
+    groups = pl.num_programs(1)
+    me = me_ref[0]
+    width = heads * HD
+
+    @pl.when((s_id == 0) & (g == 0))
+    def _():
+        acc[...] = jnp.zeros_like(acc)
+
     for k in range(n):
         d = lax.bitwise_xor(jnp.int32(k), me)
-        outs[k][0] = res[d]
-
-
-def close_kernel(n, heads, slices, me_ref, pack_ref, *refs):
+
+        @pl.when(d // heads == g)
+        def _():
+            scr[d % heads] = recv[k][0]
+
+    @pl.when(pack_ref[g, s_id] < pack_ref[groups, 0])
+    def _():
+        attended = scr[...].reshape(width, c_ref.shape[1])
+        acc[...] += dot(attended, c_ref[0])
+        branch = dot(attended.T, merge_ref[...]) + branch_ref[0].astype(F32)
+        cols = branch.shape[1] // slices
+        for m in range(slices):
+            out_branch[m, 0] = branch[:, m * cols : (m + 1) * cols].astype(BF16)
+
+    @pl.when((s_id == pl.num_programs(0) - 1) & (g == groups - 1))
+    def _():
+        out_weight[...] = acc[...].astype(BF16)
+
+
+def close_kernel(n, heads, me_ref, pack_ref, *refs):
     recv = refs[:n]
-    normed_ref, c_ref, w_ref, merge_ref, cos_ref, sin_ref, branch_ref, low_ref = refs[n : n + 8]
-    out_branch, out_low, out_weight, scr, acc = refs[n + 8 :]
+    normed_ref, w_ref, cos_ref, sin_ref, low_ref, out_low, out_weight, scr, acc = refs[n:]
     s_id, g = pl.program_id(0), pl.program_id(1)
     groups = pl.num_programs(1)
     me = me_ref[0]
@@ -188,26 +275,20 @@
 
         @pl.when(d // heads == g)
         def _():
-            for j in range(4):
+            for j in range(3):
                 scr[j, d % heads] = recv[k][0, j]
 
     @pl.when(pack_ref[g, s_id] < pack_ref[groups, 0])
     def _():
-        attended = scr[0].reshape(width, shard)
         parts = []
-        for j in (1, 2):
+        for j in (0, 1):
             part = scr[j].reshape(width, shard).astype(F32)
             parts.append(turn(part, cos_ref[0], -sin_ref[0], heads).astype(BF16))
-        parts.append(scr[3].reshape(width, shard))
+        parts.append(scr[2].reshape(width, shard))
         grads = jnp.concatenate(parts, axis=0)
-        acc[: 3 * width] += dot(grads, normed_ref[0])
-        acc[3 * width :] += dot(attended, c_ref[0])
+        acc[...] += dot(grads, normed_ref[0])
         low = dot(grads.T, w_ref[...]) + low_ref[0].astype(F32)
         out_low[0] = low.astype(BF16)
-        branch = dot(attended.T, merge_ref[...]) + branch_ref[0].astype(F32)
-        cols = branch.shape[1] // slices
-        for m in range(slices):
-            out_branch[m, 0] = branch[:, m * cols : (m + 1) * cols].astype(BF16)
 
     @pl.when((s_id == pl.num_programs(0) - 1) & (g == groups - 1))
     def _():
@@ -224,6 +305,43 @@
     for k in range(1, n):
         out.append(lax.ppermute(parts[k], "seq", [(i, i ^ k) for i in range(n)]))
     return out
+
+
+def span(masks):
+    out = [0]
+    for m in masks:
+        out += [v ^ m for v in out]
+    return out
+
+
+def cube_sum(chunks, axis, masks, kind):
+    n = len(chunks)
+    chunks = dict(enumerate(chunks))
+    for step, m in enumerate(masks):
+        kept = span(masks[step + 1 :])
+        sent = jnp.stack([chunks[k ^ m] for k in kept]).astype(kind)
+        got = lax.ppermute(sent, axis, [(i, i ^ m) for i in range(n)])
+        chunks = {
+            k: chunks[k].astype(F32) + got[at].astype(F32) for at, k in enumerate(kept)
+        }
+    return chunks[0]
+
+
+def masks_of(n):
+    return [1, 2, 6] if n == 8 else [1 << b for b in range(n.bit_length() - 1)]
+
+
+def turned(masks, by):
+    by = by % len(masks)
+    return masks[by:] + masks[:by]
+
+
+def cut(array, axis, n, me):
+    size = array.shape[axis] // n
+    return [
+        lax.dynamic_slice_in_dim(array, lax.bitwise_xor(jnp.int32(k), me) * size, size, axis)
+        for k in range(n)
+    ]
 
 
 def on_device(
@@ -369,8 +487,31 @@
         "psd,psf->df", normed_low, hidden_grad, preferred_element_type=F32
     ).astype(BF16)
     down_grad = jnp.einsum("psd,psf->df", cot, active_low, preferred_element_type=F32).astype(BF16)
-    up_grad = lax.psum_scatter(up_grad, "seq", scatter_dimension=0, tiled=True)
-    down_grad = lax.psum_scatter(down_grad, "seq", scatter_dimension=0, tiled=True)
+    seq_masks = masks_of(n)
+    up_cut, down_cut = cut(up_grad, 0, n, rank), cut(down_grad, 0, n, rank)
+    both = [jnp.concatenate(pair, axis=1) for pair in zip(up_cut, down_cut)]
+    third = both[0].shape[1] // 384 * 128
+    edges = [0, third, 2 * third, both[0].shape[1]]
+    both = jnp.concatenate(
+        [
+            cube_sum([v[:, lo:hi] for v in both], "seq", turned(seq_masks, r), BF16)
+            for r, (lo, hi) in enumerate(zip(edges, edges[1:]))
+        ],
+        axis=1,
+    )
+    hidden_here = up_weight.shape[1]
+    up_grad, down_grad = both[:, :hidden_here], both[:, hidden_here:].T
+    biases = cube_sum(
+        [
+            jnp.concatenate(pair)
+            for pair in zip(cut(up_bias_grad, 0, n, rank), cut(down_bias_grad, 0, n, rank))
+        ],
+        "seq",
+        seq_masks,
+        F32,
+    )
+    up_bias_grad = biases[: hidden_here // n]
+    down_bias_grad = biases[hidden_here // n :]
 
     my_packs = lax.dynamic_slice_in_dim(pack_at, rank // heads, 1, 0)[0]
     safe = jnp.minimum(my_packs, packs - 1)
@@ -380,84 +521,123 @@
     )
     chunk_spec = pl.BlockSpec((1, 3, HD, shard), lambda s, a, b, c: (s, 0, 0, 0))
     grad_spec = pl.BlockSpec((1, HD, shard), lambda s, a, b, c: (s, 0, 0))
-    backs = pl.pallas_call(
+    first_spec = pl.BlockSpec((1, n, shard), lambda s, a, b, c: (b[s], 0, 0))
+    row_chunk = pl.BlockSpec((1, n, shard), lambda s, a, b, c: (s, 0, 0))
+    keep_spec = pl.BlockSpec((1, n, HD, shard), lambda s, a, b, c: (s, 0, 0, 0))
+    first = first.reshape(packs, n, shard)
+    wide = [pltpu.VMEM((n, HD, shard), BF16)]
+    tall = [pltpu.VMEM((n, shard, HD), BF16)]
+    outs = pl.pallas_call(
         functools.partial(attend_kernel, n, shard),
         grid_spec=pltpu.PrefetchScalarGridSpec(
             num_scalar_prefetch=3,
             grid=(slots,),
-            in_specs=[pl.BlockSpec((1, n, shard), lambda s, a, b, c: (b[s], 0, 0))]
-            + [chunk_spec] * n
-            + [grad_spec] * n,
-            out_specs=[pl.BlockSpec((1, 4, HD, shard), lambda s, a, b, c: (s, 0, 0, 0))] * n,
-            scratch_shapes=[pltpu.VMEM((n, HD, shard), BF16)] * 4
-            + [pltpu.VMEM((n, shard, HD), BF16)] * 4
-            + [pltpu.VMEM((n, shard, HD), F32)] * 2
-            + [pltpu.VMEM((n, 4, HD, shard), BF16)],
-        ),
-        out_shape=[jax.ShapeDtypeStruct((slots, 4, HD, shard), BF16)] * n,
+            in_specs=[first_spec] + [chunk_spec] * n,
+            out_specs=[grad_spec] * n + [keep_spec, row_chunk],
+            scratch_shapes=wide * 2 + tall,
+        ),
+        out_shape=[jax.ShapeDtypeStruct((slots, HD, shard), BF16)] * n
+        + [
+            jax.ShapeDtypeStruct((slots, n, HD, shard), BF16),
+            jax.ShapeDtypeStruct((slots, n, shard), F32),
+        ],
         compiler_params=params(),
         cost_estimate=pl.CostEstimate(
-            flops=slots * pack_len * pack_len * HD * 14,
+            flops=slots * pack_len * pack_len * HD * 8,
+            bytes_accessed=slots * pack_len * HD * 10,
+            transcendentals=slots * pack_len * pack_len // 4,
+        ),
+        name="attend",
+    )(me, safe, lows, first, *qkv)
+    kept, logsum = outs[n], outs[n + 1]
+    attended = swap(outs[:n])
+    backs = pl.pallas_call(
+        functools.partial(attend_back_kernel, n, shard),
+        grid_spec=pltpu.PrefetchScalarGridSpec(
+            num_scalar_prefetch=3,
+            grid=(slots,),
+            in_specs=[first_spec, keep_spec, row_chunk] + [chunk_spec] * n + [grad_spec] * n,
+            out_specs=[chunk_spec] * n,
+            scratch_shapes=wide * 3
+            + tall * 4
+            + [pltpu.VMEM((n, shard, HD), F32)] * 2
+            + [pltpu.VMEM((n, 3, HD, shard), BF16)],
+        ),
+        out_shape=[jax.ShapeDtypeStruct((slots, 3, HD, shard), BF16)] * n,
+        compiler_params=params(),
+        cost_estimate=pl.CostEstimate(
+            flops=slots * pack_len * pack_len * HD * 16,
             bytes_accessed=slots * pack_len * HD * 16,
-            transcendentals=slots * pack_len * pack_len,
-        ),
-        name="attend",
-    )(me, safe, lows, first.reshape(packs, n, shard), *qkv, *grads)
+            transcendentals=slots * pack_len * pack_len // 4,
+        ),
+        name="attend_back",
+    )(me, safe, lows, first, kept, logsum, *qkv, *grads)
     backs = swap(backs)
 
-    branch, low, weight = pl.pallas_call(
-        functools.partial(close_kernel, n, heads, slices),
+    branch, merge_part = pl.pallas_call(
+        functools.partial(merge_kernel, n, heads, slices),
         grid_spec=pltpu.PrefetchScalarGridSpec(
             num_scalar_prefetch=2,
             grid=(slots, groups),
-            in_specs=[pl.BlockSpec((1, 4, HD, shard), lambda s, g, a, b: (s, 0, 0, 0))] * n
-            + [
-                row_spec,
-                row_spec,
-                pl.BlockSpec((3 * joined, width), whole2),
-                pl.BlockSpec((joined, width), whole2),
-                table_spec,
-                table_spec,
-                row_spec,
-                row_spec,
-            ],
+            in_specs=[pl.BlockSpec((1, HD, shard), lambda s, g, a, b: (s, 0, 0))] * n
+            + [row_spec, pl.BlockSpec((joined, width), whole2), row_spec],
             out_specs=[
                 pl.BlockSpec(
                     (slices, 1, shard, width // slices), lambda s, g, a, b: (0, b[g, s], 0, 0)
                 ),
-                pl.BlockSpec((1, shard, width), pack_out),
-                pl.BlockSpec((4 * joined, width), whole2),
+                pl.BlockSpec((joined, width), whole2),
             ],
             scratch_shapes=[
-                pltpu.VMEM((4, heads, HD, shard), BF16),
-                pltpu.VMEM((4 * joined, width), F32),
+                pltpu.VMEM((heads, HD, shard), BF16),
+                pltpu.VMEM((joined, width), F32),
             ],
         ),
         out_shape=[
             jax.ShapeDtypeStruct((slices, packs + spare, shard, width // slices), BF16),
-            jax.ShapeDtypeStruct((packs + spare, shard, width), BF16),
-            jax.ShapeDtypeStruct((4 * joined, width), BF16),
+            jax.ShapeDtypeStruct((joined, width), BF16),
         ],
         compiler_params=params(),
         cost_estimate=pl.CostEstimate(
-            flops=16 * rows * width * joined,
-            bytes_accessed=rows * width * 12 + rows * joined * 8,
+            flops=4 * rows * width * joined,
+            bytes_accessed=rows * width * 6 + rows * joined * 2,
             transcendentals=0,
         ),
+        name="merge",
+    )(me, pack_table, *attended, cot, merge_weight, branch_ff)
+    low, head_part = pl.pallas_call(
+        functools.partial(close_kernel, n, heads),
+        grid_spec=pltpu.PrefetchScalarGridSpec(
+            num_scalar_prefetch=2,
+            grid=(slots, groups),
+            in_specs=[pl.BlockSpec((1, 3, HD, shard), lambda s, g, a, b: (s, 0, 0, 0))] * n
+            + [
+                row_spec,
+                pl.BlockSpec((3 * joined, width), whole2),
+                table_spec,
+                table_spec,
+                row_spec,
+            ],
+            out_specs=[
+                pl.BlockSpec((1, shard, width), pack_out),
+                pl.BlockSpec((3 * joined, width), whole2),
+            ],
+            scratch_shapes=[
+                pltpu.VMEM((3, heads, HD, shard), BF16),
+                pltpu.VMEM((3 * joined, width), F32),
+            ],
+        ),
+        out_shape=[
+            jax.ShapeDtypeStruct((packs + spare, shard, width), BF16),
+            jax.ShapeDtypeStruct((3 * joined, width), BF16),
+        ],
+        compiler_params=params(),
+        cost_estimate=pl.CostEstimate(
+            flops=12 * rows * width * joined,
+            bytes_accessed=rows * width * 6 + rows * joined * 6,
+            transcendentals=0,
+        ),
         name="close",
-    )(
-        me,
-        pack_table,
-        *backs,
-        normed_low,
-        cot,
-        w_t,
-        merge_weight,
-        cosine,
-        sine,
-        branch_ff,
-        low_ff,
-    )
+    )(me, pack_table, *backs, normed_low, w_t, cosine, sine, low_ff)
     branch = branch[:, :packs]
     low = low[:packs]
     summed = lax.psum_scatter(branch, "mlp", scatter_dimension=0, tiled=False)
@@ -469,9 +649,9 @@
     ).astype(BF16)
 
     share = rows // slices
-    low_sum = lax.psum_scatter(
-        low.reshape(rows, width), "mlp", scatter_dimension=0, tiled=True
-    ).astype(F32)
+    low_sum = cube_sum(
+        cut(low.reshape(rows, width), 0, slices, column), "mlp", masks_of(slices), BF16
+    )
     row_in = lax.dynamic_slice_in_dim(
         tokens.reshape(rows, width), column * share, share, 0
     ).astype(F32)
@@ -492,18 +672,23 @@
         * inverse
     ).astype(BF16)
     tokens_grad = lax.all_gather(row_grad, "mlp", axis=0, tiled=True).reshape(packs, shard, width)
-    gain_grad = lax.psum(jnp.sum(low_sum * xhat, axis=0), "mlp")
-    shift_grad = lax.psum(jnp.sum(low_sum, axis=0), "mlp")
-
-    weight = lax.psum_scatter(weight, "seq", scatter_dimension=1, tiled=True).astype(F32)
-    part = width // n
-    head_grad = jnp.transpose(weight[: 3 * joined].reshape(3, joined, part), (0, 2, 1))
-    merge_grad = weight[3 * joined :]
-    gain_grad, shift_grad, up_bias_grad, down_bias_grad = (
-        lax.psum_scatter(gain_grad, "seq", scatter_dimension=0, tiled=True),
-        lax.psum_scatter(shift_grad, "seq", scatter_dimension=0, tiled=True),
-        lax.psum_scatter(up_bias_grad, "seq", scatter_dimension=0, tiled=True),
-        lax.psum_scatter(down_bias_grad, "seq", scatter_dimension=0, tiled=True),
+    vectors = jnp.stack([jnp.sum(low_sum * xhat, axis=0), jnp.sum(low_sum, axis=0)])
+    vectors = cube_sum(cut(vectors, 1, n, rank), "seq", seq_masks, F32)
+    for m in masks_of(slices):
+        vectors = vectors + lax.ppermute(vectors, "mlp", [(i, i ^ m) for i in range(slices)])
+    gain_grad, shift_grad = vectors[0], vectors[1]
+
+    merge_grad = cube_sum(cut(merge_part, 1, n, rank), "seq", seq_masks, BF16)
+    head_grad = jnp.stack(
+        [
+            cube_sum(
+                cut(head_part[j * joined : (j + 1) * joined], 1, n, rank),
+                "seq",
+                turned(seq_masks, j),
+                BF16,
+            ).T
+            for j in range(3)
+        ]
     )
     return (
         result,
@@ -512,9 +697,9 @@
         shift_grad,
         head_grad,
         merge_grad,
-        up_grad.astype(F32),
+        up_grad,
         up_bias_grad,
-        down_grad.astype(F32).T,
+        down_grad,
         down_bias_grad,
     )
 

time: 879 us -> 655 us (0.75)
  the two profiles are of different devices: /device:TPU:17 before, /device:TPU:0 now
where the time goes in v2:
time: 655 us; the launch traced here: 642 us
  waiting for transfers between devices  179 us (27%)
  Pallas kernels  162 us (25%)
  starting transfers between devices  154 us (24%)
  matrix products  67.9 us (10%)
  other arithmetic  38.9 us (6%)
  local copies, waits for them, and re-layouts  25.6 us (4%)
  between operations  15 us (2%)
    ppermute x28, waiting for transfers between devices, swap(): out.append(lax.ppermute(parts[k], 'seq', [(i, i ^ k) for i in range(n)]))  116 us
    ppermute x28, starting transfers between devices, swap(): out.append(lax.ppermute(parts[k], 'seq', [(i, i ^ k) for i in range(n)]))  87 us
    ppermute x29, starting transfers between devices, cube_sum(): got = lax.ppermute(sent, axis, [(i, i ^ m) for i in range(n)])  65 us
    ppermute x29, waiting for transfers between devices, cube_sum(): got = lax.ppermute(sent, axis, [(i, i ^ m) for i in range(n)])  62 us
    pallas_call x1, Pallas kernels, on_device(): pl.pallas_call(functools.partial(attend_back_kernel, n, shard), grid_spec...  53.7 us
    pallas_call x1, Pallas kernels, on_device(): pl.pallas_call(functools.partial(attend_kernel, n, shard), grid_spec=pltp...  41.5 us
    pallas_call x1, Pallas kernels, on_device(): pl.pallas_call(functools.partial(close_kernel, n, heads), grid_spec=pltpu...  21.4 us
    pallas_call x1, Pallas kernels, on_device(): pl.pallas_call(functools.partial(head_kernel, n, heads), grid_spec=pltpu....  19 us
  transfers between devices with their start and end apart: 62, of which 22 were waited for; matrix products, arithmetic and copies ran while one was open for 19% of the time, Pallas kernels for 25%

profile of v2, /device:TPU:0, one launch (start us, length us, event | category | flops | bytes accessed | tf_op | source)
XLA Modules:
  0.0 642.1 jit_solution(13869295012307569781)
XLA Ops:
  10.8 2.6 copy.52
  17.7 19.0 %heads.1 = (bf16[12,256,1024]{2,1,0:T(8,128)(2,1)}, bf16[6,3,64,256]{3,2,1,0:T(8,128)(2,1)}, bf16[6,3,64,256]{3,2,1,0:T(8,128)(2,1)}, bf16[6,3,64,256]{3,2,1,0:T...) custom-call(s32[1]{0:T(128)} %bitcast.me_ref, ...), custom_call_target="tpu_custom_call" | custom-call | flops 4831838208 | bytes 17301504 | tf_op jit(solution)/shard_map/heads/pallas_call | solution.py:412
  36.7 3.0 collective-permute-start
  41.3 3.0 collective-permute-start.3
  45.6 9.0 %fusion.25 = f32[12,256,1024]{2,1,0:T(8,128)S(1)} fusion(bf16[12,256,1024]{2,1,0:T(8,128)(2,1)} %get-tuple-element.65.refs_8_, bf16[1024,1024]{1,0:T(8,128)(2,1)S(1)} %copy-done.17), kind=kOutput, calls=%fused_computation.43 | convolution fusion | flops 6442450944 | bytes 20971520 | tf_op jit(solution)/shard_map/psd,df->psf/dot_general | solution.py:472
  54.7 10.4 %convolution_convert_fusion.1.refs_10_ = bf16[12,256,1024]{2,1,0:T(8,128)(2,1)} fusion(bf16[1024,1024]{1,0:T(8,128)(2,1)S(1)} %copy-done, f32[12,256,1024]{2,1,0:T(8,128)S(1)} %fusion.25, f32[1024]{0:T(1024)S(1)} %copy-done.40), kind=kOutput, calls=%fused_computation.23 | convolution fusion | flops 6477053952 | bytes 20975616 | tf_op jit(solution)/shard_map/psf,fd->psd/dot_general | solution.py:480
  66.5 3.7 collective-permute-start.5
  70.2 10.5 %collective-permute-done.1.refs_2_.refs_4_ = bf16[6,3,64,256]{3,2,1,0:T(8,128)(2,1)S(1)} collective-permute-done((bf16[6,3,64,256]{3,2,1,0:T(8,128)(2,1)}, bf16[6,3,64,256]{3,2,1,0:T(8,128)(2,1)S(1)}, u32[]{:S(2)}, u32[]{:S(2)}) %collective-permute-start.1) | collective-permute-done | bytes 589856 | tf_op jit(solution)/shard_map/ppermute | solution.py:306
  84.0 6.9 %collective-permute-done.2.refs_3_.refs_5_ = bf16[6,3,64,256]{3,2,1,0:T(8,128)(2,1)} collective-permute-done((bf16[6,3,64,256]{3,2,1,0:T(8,128)(2,1)}, bf16[6,3,64,256]{3,2,1,0:T(8,128)(2,1)}, u32[]{:S(2)}, u32[]{:S(2)}) %collective-permute-start.2) | collective-permute-done | bytes 589856 | tf_op jit(solution)/shard_map/ppermute | solution.py:306
  91.0 32.3 %collective-permute-done.4.refs_5_.refs_7_ = bf16[6,3,64,256]{3,2,1,0:T(8,128)(2,1)} collective-permute-done((bf16[6,3,64,256]{3,2,1,0:T(8,128)(2,1)}, bf16[6,3,64,256]{3,2,1,0:T(8,128)(2,1)}, u32[]{:S(2)}, u32[]{:S(2)}) %collective-permute-start.4) | collective-permute-done | bytes 589856 | tf_op jit(solution)/shard_map/ppermute | solution.py:306
  124.3 41.5 %attend.1 = (bf16[6,64,256]{2,1,0:T(8,128)(2,1)}, bf16[6,64,256]{2,1,0:T(8,128)(2,1)}, bf16[6,64,256]{2,1,0:T(8,128)(2,1)}, bf16[6,64,256]{2,1,0:T(8,128)(2,1)},...) custom-call(s32[1]{0:T(128)} %bitcast.me_ref, ...), custom_call_target="tpu_custom_call" | custom-call | flops 12884901888 | bytes 7864320 | tf_op jit(solution)/shard_map/attend/pallas_call | solution.py:530
  165.9 24.4 %collective-permute-start.8 = (bf16[6,64,256]{2,1,0:T(8,128)(2,1)}, bf16[6,64,256]{2,1,0:T(8,128)(2,1)S(1)}, u32[]{:S(2)}, u32[]{:S(2)}) collective-permute-start(bf16[6,64,256]{2,1,0:T(8,128)(2,1)} %get-tuple-element.59), channel_id=1, source_target_pairs={{0,8},{4,12},{8,0},{12,4},{16,24},{20,28},{24,16},{28,20},{1,9},{5... | collective-permute-start | bytes 589832 | tf_op jit(solution)/shard_map/ppermute | solution.py:306
  190.9 2.7 collective-permute-start.10
  197.5 11.8 %out_grads.1 = (bf16[6,64,256]{2,1,0:T(8,128)(2,1)}, bf16[6,64,256]{2,1,0:T(8,128)(2,1)}, bf16[6,64,256]{2,1,0:T(8,128)(2,1)}, bf16[6,64,256]{2,1,0:T(8,128)(2,1...) custom-call(s32[1]{0:T(128)} %bitcast.me_ref, ...), custom_call_target="tpu_custom_call" | custom-call | flops 1610612736 | bytes 7864320 | tf_op jit(solution)/shard_map/out_grads/pallas_call | solution.py:451
  211.2 2.6 collective-permute-start.13
  219.0 5.7 collective-permute-start.17
  224.8 7.0 %collective-permute-start.18 = (bf16[6,64,256]{2,1,0:T(8,128)(2,1)}, bf16[6,64,256]{2,1,0:T(8,128)(2,1)S(1)}, u32[]{:S(2)}, u32[]{:S(2)}) collective-permute-start(bf16[6,64,256]{2,1,0:T(8,128)(2,1)} %get-tuple-element.74), channel_id=1, source_target_pairs={{0,20},{4,16},{8,28},{12,24},{16,4},{20,0},{24,12},{28,8},{1,21},{... | collective-permute-start | bytes 589832 | tf_op jit(solution)/shard_map/ppermute | solution.py:306
  231.7 4.4 collective-permute-start.19
  238.6 14.9 %merge.1 = (bf16[4,12,256,256]{3,2,1,0:T(8,128)(2,1)}, bf16[256,1024]{1,0:T(8,128)(2,1)}) custom-call(s32[1]{0:T(128)} %bitcast.me_ref, s32[3,6]{1,0:T(4,128)} %concatenate.73.pack_ref, bf16[6,64,256]{2,1,0:T(8,128)(2,1)} %get-tuple-element.57.refs_0_, bf16[6,64,256]{2,1,0:T(8,128)(2,1)} %copy-done.8, bf16[6,64,256]{2,1,0:T(8,128)(2,1)} %copy-done.9, ...), custom_call_target="tpu_custom_call" | custom-call | flops 3221225472 | bytes 20447232 | tf_op jit(solution)/shard_map/merge/pallas_call | solution.py:577
  254.4 53.7 %attend_back.1 = (bf16[6,3,64,256]{3,2,1,0:T(8,128)(2,1)}, bf16[6,3,64,256]{3,2,1,0:T(8,128)(2,1)}, bf16[6,3,64,256]{3,2,1,0:T(8,128)(2,1)}, bf16[6,3,64,256]{3,...) custom-call(s32[1]{0:T(128)} %bitcast.me_ref, ...), custom_call_target="tpu_custom_call" | custom-call | flops 25769803776 | bytes 12582912 | tf_op jit(solution)/shard_map/attend_back/pallas_call | solution.py:554
  309.4 8.1 %collective-permute-start.22 = (bf16[6,3,64,256]{3,2,1,0:T(8,128)(2,1)}, bf16[6,3,64,256]{3,2,1,0:T(8,128)(2,1)S(1)}, u32[]{:S(2)}, u32[]{:S(2)}) collective-permute-start(bf16[6,3,64,256]{3,2,1,0:T(8,128)(2,1)} %get-tuple-element.79), channel_id=1, source_target_pairs={{0,8},{4,12},{8,0},{12,4},{16,24},{20,28},{24,16},{28,20},{1,9},{5... | collective-permute-start | bytes 1769480 | tf_op jit(solution)/shard_map/ppermute | solution.py:306
  317.5 18.3 %convert_reduce_fusion.1 = (f32[1024]{0:T(1024)S(1)}, bf16[12,256,1024]{2,1,0:T(8,128)(2,1)S(1)}) fusion(f32[12,256,1024]{2,1,0:T(8,128)} %copy-done.41, f32[1024]{0:T(1024)S(1)} %copy-done.40, bf16[12,256,1024]{2,1,0:T(8,128)(2,1)} %all-gather.3.cloned.1.call-done.refs_8_.c_ref, bf16[1024,1024]{1,0:T(8,128)(2,1)S(1)} %copy-done), kind=kOutput, calls=%fused_computation.11 | convolution fusion | flops 6514801664 | bytes 27271168 | tf_op jit(solution)/shard_map/psd,fd->psf/dot_general | solution.py:475
  337.0 2.8 collective-permute-start.25
  341.3 2.8 collective-permute-start.27
  344.1 9.0 %convolution_convert_fusion.refs_12_ = bf16[12,256,1024]{2,1,0:T(8,128)(2,1)} fusion(bf16[12,256,1024]{2,1,0:T(8,128)(2,1)S(1)} %get-tuple-element.218, bf16[1024,1024]{1,0:T(8,128)(2,1)S(1)} %copy-done.18), kind=kOutput, calls=%fused_computation.22 | convolution fusion | flops 6445596672 | bytes 14680064 | tf_op jit(solution)/shard_map/psf,df->psd/dot_general | solution.py:483
  353.1 8.2 %collective-permute-done.23.refs_3_ = bf16[6,3,64,256]{3,2,1,0:T(8,128)(2,1)S(1)} collective-permute-done((bf16[6,3,64,256]{3,2,1,0:T(8,128)(2,1)S(1)}, bf16[6,3,64,256]{3,2,1,0:T(8,128)(2,1)S(1)}, u32[]{:S(2)}, u32[]{:S(2)}) %collective-permute-start.23) | collective-permute-done | bytes 589856 | tf_op jit(solution)/shard_map/ppermute | solution.py:306
  361.3 42.8 %collective-permute-done.24.refs_4_ = bf16[6,3,64,256]{3,2,1,0:T(8,128)(2,1)S(1)} collective-permute-done((bf16[6,3,64,256]{3,2,1,0:T(8,128)(2,1)S(1)}, bf16[6,3,64,256]{3,2,1,0:T(8,128)(2,1)S(1)}, u32[]{:S(2)}, u32[]{:S(2)}) %collective-permute-start.24) | collective-permute-done | bytes 589856 | tf_op jit(solution)/shard_map/ppermute | solution.py:306
  404.1 13.2 %collective-permute-done.25.refs_5_ = bf16[6,3,64,256]{3,2,1,0:T(8,128)(2,1)S(1)} collective-permute-done((bf16[6,3,64,256]{3,2,1,0:T(8,128)(2,1)S(1)}, bf16[6,3,64,256]{3,2,1,0:T(8,128)(2,1)S(1)}, u32[]{:S(2)}, u32[]{:S(2)}) %collective-permute-start.25) | collective-permute-done | bytes 589856 | tf_op jit(solution)/shard_map/ppermute | solution.py:306
  419.0 21.4 %close.1 = (bf16[12,256,1024]{2,1,0:T(8,128)(2,1)}, bf16[768,1024]{1,0:T(8,128)(2,1)}) custom-call(s32[1]{0:T(128)} %bitcast.me_ref, s32[3,6]{1,0:T(4,128)} %concatenate.73.pack_ref, bf16[6,3,64,256]{3,2,1,0:T(8,128)(2,1)} %get-tuple-element.77.refs_0_, bf16[6,3,64,256]{3,2,1,0:T(8,128)(2,1)} %copy-done.28, bf16[6,3,64,256]{3,2,1,0:T(8,128)(2,1)} %copy-done.29, ...), custom_call_target="tpu_custom_call" | custom-call | flops 9663676416 | bytes 23592960 | tf_op jit(solution)/shard_map/close/pallas_call | solution.py:607
  444.2 10.4 %bitcast_convert_fusion = bf16[1024,1024]{1,0:T(8,128)(2,1)S(1)} fusion(bf16[12,256,1024]{2,1,0:T(8,128)(2,1)S(1)} %bitcast.523, f32[12,256,1024]{2,1,0:T(8,128)} %copy-done.41, f32[1024]{0:T(1024)S(1)} %copy-done.40), kind=kOutput, calls=%fused_computation.13 | convolution fusion | flops 6474956800 | bytes 20975616 | tf_op jit(solution)/shard_map/psd,psf->df/dot_general | solution.py:489
  458.4 10.8 %bitcast_convert_fusion.1 = bf16[1024,1024]{0,1:T(8,128)(2,1)S(1)} fusion(bf16[12,256,1024]{2,1,0:T(8,128)(2,1)} %get-tuple-element.65.refs_8_, bf16[12,256,1024]{2,1,0:T(8,128)(2,1)} %copy-done.42), kind=kOutput, calls=%fused_computation.14 | convolution fusion | flops 6443499520 | bytes 14680064 | tf_op jit(solution)/shard_map/psd,psf->df/dot_general | solution.py:486
  479.6 25.9 %collective-permute-done.29 = bf16[1,768,1024]{2,1,0:T(8,128)(2,1)S(1)} collective-permute-done((bf16[1,768,1024]{2,1,0:T(8,128)(2,1)S(1)}, bf16[1,768,1024]{2,1,0:T(8,128)(2,1)S(1)}, u32[]{:S(2)}, u32[]{:S(2)}) %collective-permute-start.29) | collective-permute-done | bytes 1572896 | tf_op jit(solution)/shard_map/ppermute | solution.py:323
  510.6 22.0 %collective-permute-start.54 = (f32[2,256]{1,0:T(2,128)S(1)}, f32[2,256]{1,0:T(2,128)S(1)}, u32[]{:S(2)}, u32[]{:S(2)}) collective-permute-start(f32[2,256]{1,0:T(2,128)S(1)} %pad_maximum_fusion.29), channel_id=1, source_target_pairs={{0,8},{4,12},{8,0},{12,4},{16,24},{20,28},{24,16},{28,20},{1,9},{5... | collective-permute-start | bytes 6152 | tf_op jit(solution)/shard_map/ppermute | solution.py:323
  534.2 2.6 collective-permute-start.55
  539.1 11.8 %collective-permute-done.55 = f32[1,256]{1,0:T(1,128)S(1)} collective-permute-done((f32[1,256]{1,0:T(1,128)S(1)}, f32[1,256]{1,0:T(1,128)S(1)}, u32[]{:S(2)}, u32[]{:S(2)}) %collective-permute-start.55) | collective-permute-done | bytes 1056 | tf_op jit(solution)/shard_map/ppermute | solution.py:323
  552.4 2.6 collective-permute-start.46
  555.5 3.0 collective-permute-done.46
  562.4 2.6 collective-permute-start.51
  570.3 5.4 collective-permute-done.48
  579.7 3.7 collective-permute-start.49
  586.1 3.1 collective-permute-done.41
  589.3 4.4 collective-permute-start.39
  595.0 4.4 collective-permute-start.36
  608.5 2.6 collective-permute-done.30
  612.0 2.8 collective-permute-done.31
  617.2 3.0 collective-permute-done.32
  625.5 3.5 fusion.21
  629.0 6.3 copy.66
  (311 shorter events, 100.2 us)
Async XLA Ops:
  7.2 190.3 %all-gather.3.cloned.1.call-start = ((), (), s32[]{:S(2)}) async-start(), calls=%async_computation.1 | async-start | bytes 7864320 | tf_op jit(solution)/shard_map/all_gather | solution.py:374
  7.9 617.6 %reduce-scatter.2.cloned.1.call-start = ((), (), s32[]{:S(2)}) async-start(), calls=%async_computation.2 | async-start | bytes 7864320 | tf_op jit(solution)/shard_map/reduce_scatter | solution.py:643
  36.7 29.8 %collective-permute-start = (bf16[6,3,64,256]{3,2,1,0:T(8,128)(2,1)}, bf16[6,3,64,256]{3,2,1,0:T(8,128)(2,1)S(1)}, u32[]{:S(2)}, u32[]{:S(2)}) collective-permute-start(bf16[6,3,64,256]{3,2,1,0:T(8,128)(2,1)} %get-tuple-element.50), channel_id=1, source_target_pairs={{0,4},{4,0},{8,12},{12,8},{16,20},{20,16},{24,28},{28,24},{1,5},{5... | collective-permute-start | bytes 1769480 | tf_op jit(solution)/shard_map/ppermute | solution.py:306
  39.7 41.0 %collective-permute-start.1 = (bf16[6,3,64,256]{3,2,1,0:T(8,128)(2,1)}, bf16[6,3,64,256]{3,2,1,0:T(8,128)(2,1)S(1)}, u32[]{:S(2)}, u32[]{:S(2)}) collective-permute-start(bf16[6,3,64,256]{3,2,1,0:T(8,128)(2,1)} %get-tuple-element.51), channel_id=1, source_target_pairs={{0,8},{4,12},{8,0},{12,4},{16,24},{20,28},{24,16},{28,20},{1,9},{5... | collective-permute-start | bytes 1769480 | tf_op jit(solution)/shard_map/ppermute | solution.py:306
  41.3 49.6 %collective-permute-start.2 = (bf16[6,3,64,256]{3,2,1,0:T(8,128)(2,1)}, bf16[6,3,64,256]{3,2,1,0:T(8,128)(2,1)}, u32[]{:S(2)}, u32[]{:S(2)}) collective-permute-start(bf16[6,3,64,256]{3,2,1,0:T(8,128)(2,1)} %get-tuple-element.52), channel_id=1, source_target_pairs={{0,12},{4,8},{8,4},{12,0},{16,28},{20,24},{24,20},{28,16},{1,13},{... | collective-permute-start | bytes 1769480 | tf_op jit(solution)/shard_map/ppermute | solution.py:306
  41.3 49.6 %collective-permute-start.3 = (bf16[6,3,64,256]{3,2,1,0:T(8,128)(2,1)}, bf16[6,3,64,256]{3,2,1,0:T(8,128)(2,1)}, u32[]{:S(2)}, u32[]{:S(2)}) collective-permute-start(bf16[6,3,64,256]{3,2,1,0:T(8,128)(2,1)} %get-tuple-element.53), channel_id=1, source_target_pairs={{0,16},{4,20},{8,24},{12,28},{16,0},{20,4},{24,8},{28,12},{1,17},{... | collective-permute-start | bytes 1769480 | tf_op jit(solution)/shard_map/ppermute | solution.py:306
  44.3 79.0 %collective-permute-start.4 = (bf16[6,3,64,256]{3,2,1,0:T(8,128)(2,1)}, bf16[6,3,64,256]{3,2,1,0:T(8,128)(2,1)}, u32[]{:S(2)}, u32[]{:S(2)}) collective-permute-start(bf16[6,3,64,256]{3,2,1,0:T(8,128)(2,1)} %get-tuple-element.54), channel_id=1, source_target_pairs={{0,20},{4,16},{8,28},{12,24},{16,4},{20,0},{24,12},{28,8},{1,21},{... | collective-permute-start | bytes 1769480 | tf_op jit(solution)/shard_map/ppermute | solution.py:306
  66.5 56.8 %collective-permute-start.5 = (bf16[6,3,64,256]{3,2,1,0:T(8,128)(2,1)}, bf16[6,3,64,256]{3,2,1,0:T(8,128)(2,1)S(1)}, u32[]{:S(2)}, u32[]{:S(2)}) collective-permute-start(bf16[6,3,64,256]{3,2,1,0:T(8,128)(2,1)} %get-tuple-element.55), channel_id=1, source_target_pairs={{0,24},{4,28},{8,16},{12,20},{16,8},{20,12},{24,0},{28,4},{1,25},{... | collective-permute-start | bytes 1769480 | tf_op jit(solution)/shard_map/ppermute | solution.py:306
  80.7 42.6 %collective-permute-start.6 = (bf16[6,3,64,256]{3,2,1,0:T(8,128)(2,1)}, bf16[6,3,64,256]{3,2,1,0:T(8,128)(2,1)S(1)}, u32[]{:S(2)}, u32[]{:S(2)}) collective-permute-start(bf16[6,3,64,256]{3,2,1,0:T(8,128)(2,1)} %get-tuple-element.56), channel_id=1, source_target_pairs={{0,28},{4,24},{8,20},{12,16},{16,12},{20,8},{24,4},{28,0},{1,29},{... | collective-permute-start | bytes 1769480 | tf_op jit(solution)/shard_map/ppermute | solution.py:306
  165.8 43.5 %collective-permute-start.7 = (bf16[6,64,256]{2,1,0:T(8,128)(2,1)}, bf16[6,64,256]{2,1,0:T(8,128)(2,1)S(1)}, u32[]{:S(2)}, u32[]{:S(2)}) collective-permute-start(bf16[6,64,256]{2,1,0:T(8,128)(2,1)} %get-tuple-element.58), channel_id=1, source_target_pairs={{0,4},{4,0},{8,12},{12,8},{16,20},{20,16},{24,28},{28,24},{1,5},{5... | collective-permute-start | bytes 589832 | tf_op jit(solution)/shard_map/ppermute | solution.py:306
  165.9 45.3 %collective-permute-start.8 = (bf16[6,64,256]{2,1,0:T(8,128)(2,1)}, bf16[6,64,256]{2,1,0:T(8,128)(2,1)S(1)}, u32[]{:S(2)}, u32[]{:S(2)}) collective-permute-start(bf16[6,64,256]{2,1,0:T(8,128)(2,1)} %get-tuple-element.59), channel_id=1, source_target_pairs={{0,8},{4,12},{8,0},{12,4},{16,24},{20,28},{24,16},{28,20},{1,9},{5... | collective-permute-start | bytes 589832 | tf_op jit(solution)/shard_map/ppermute | solution.py:306
  190.3 23.6 %collective-permute-start.9 = (bf16[6,64,256]{2,1,0:T(8,128)(2,1)}, bf16[6,64,256]{2,1,0:T(8,128)(2,1)S(1)}, u32[]{:S(2)}, u32[]{:S(2)}) collective-permute-start(bf16[6,64,256]{2,1,0:T(8,128)(2,1)} %get-tuple-element.60), channel_id=1, source_target_pairs={{0,12},{4,8},{8,4},{12,0},{16,28},{20,24},{24,20},{28,16},{1,13},{... | collective-permute-start | bytes 589832 | tf_op jit(solution)/shard_map/ppermute | solution.py:306
  190.9 23.8 %collective-permute-start.10 = (bf16[6,64,256]{2,1,0:T(8,128)(2,1)}, bf16[6,64,256]{2,1,0:T(8,128)(2,1)S(1)}, u32[]{:S(2)}, u32[]{:S(2)}) collective-permute-start(bf16[6,64,256]{2,1,0:T(8,128)(2,1)} %get-tuple-element.61), channel_id=1, source_target_pairs={{0,16},{4,20},{8,24},{12,28},{16,0},{20,4},{24,8},{28,12},{1,17},{... | collective-permute-start | bytes 589832 | tf_op jit(solution)/shard_map/ppermute | solution.py:306
  197.0 18.0 %collective-permute-start.11 = (bf16[6,64,256]{2,1,0:T(8,128)(2,1)}, bf16[6,64,256]{2,1,0:T(8,128)(2,1)S(1)}, u32[]{:S(2)}, u32[]{:S(2)}) collective-permute-start(bf16[6,64,256]{2,1,0:T(8,128)(2,1)} %get-tuple-element.62), channel_id=1, source_target_pairs={{0,20},{4,16},{8,28},{12,24},{16,4},{20,0},{24,12},{28,8},{1,21},{... | collective-permute-start | bytes 589832 | tf_op jit(solution)/shard_map/ppermute | solution.py:306
  211.2 13.5 %collective-permute-start.13 = (bf16[6,64,256]{2,1,0:T(8,128)(2,1)S(1)}, bf16[6,64,256]{2,1,0:T(8,128)(2,1)S(1)}, u32[]{:S(2)}, u32[]{:S(2)}) collective-permute-start(bf16[6,64,256]{2,1,0:T(8,128)(2,1)S(1)} %copy-done.35), channel_id=1, source_target_pairs={{0,28},{4,24},{8,20},{12,16},{16,12},{20,8},{24,4},{28,0},{1,29},{... | collective-permute-start | bytes 589832 | tf_op jit(solution)/shard_map/ppermute | solution.py:306
  213.9 17.8 %collective-permute-start.14 = (bf16[6,64,256]{2,1,0:T(8,128)(2,1)}, bf16[6,64,256]{2,1,0:T(8,128)(2,1)S(1)}, u32[]{:S(2)}, u32[]{:S(2)}) collective-permute-start(bf16[6,64,256]{2,1,0:T(8,128)(2,1)} %get-tuple-element.70), channel_id=1, source_target_pairs={{0,4},{4,0},{8,12},{12,8},{16,20},{20,16},{24,28},{28,24},{1,5},{5... | collective-permute-start | bytes 589832 | tf_op jit(solution)/shard_map/ppermute | solution.py:306
  214.8 21.4 %collective-permute-start.15 = (bf16[6,64,256]{2,1,0:T(8,128)(2,1)}, bf16[6,64,256]{2,1,0:T(8,128)(2,1)S(1)}, u32[]{:S(2)}, u32[]{:S(2)}) collective-permute-start(bf16[6,64,256]{2,1,0:T(8,128)(2,1)} %get-tuple-element.71), channel_id=1, source_target_pairs={{0,8},{4,12},{8,0},{12,4},{16,24},{20,28},{24,16},{28,20},{1,9},{5... | collective-permute-start | bytes 589832 | tf_op jit(solution)/shard_map/ppermute | solution.py:306
  215.0 38.5 %collective-permute-start.16 = (bf16[6,64,256]{2,1,0:T(8,128)(2,1)}, bf16[6,64,256]{2,1,0:T(8,128)(2,1)}, u32[]{:S(2)}, u32[]{:S(2)}) collective-permute-start(bf16[6,64,256]{2,1,0:T(8,128)(2,1)} %get-tuple-element.72), channel_id=1, source_target_pairs={{0,12},{4,8},{8,4},{12,0},{16,28},{20,24},{24,20},{28,16},{1,13},{... | collective-permute-start | bytes 589832 | tf_op jit(solution)/shard_map/ppermute | solution.py:306
  219.0 34.5 %collective-permute-start.17 = (bf16[6,64,256]{2,1,0:T(8,128)(2,1)}, bf16[6,64,256]{2,1,0:T(8,128)(2,1)}, u32[]{:S(2)}, u32[]{:S(2)}) collective-permute-start(bf16[6,64,256]{2,1,0:T(8,128)(2,1)} %get-tuple-element.73), channel_id=1, source_target_pairs={{0,16},{4,20},{8,24},{12,28},{16,0},{20,4},{24,8},{28,12},{1,17},{... | collective-permute-start | bytes 589832 | tf_op jit(solution)/shard_map/ppermute | solution.py:306
  224.8 29.0 %collective-permute-start.18 = (bf16[6,64,256]{2,1,0:T(8,128)(2,1)}, bf16[6,64,256]{2,1,0:T(8,128)(2,1)S(1)}, u32[]{:S(2)}, u32[]{:S(2)}) collective-permute-start(bf16[6,64,256]{2,1,0:T(8,128)(2,1)} %get-tuple-element.74), channel_id=1, source_target_pairs={{0,20},{4,16},{8,28},{12,24},{16,4},{20,0},{24,12},{28,8},{1,21},{... | collective-permute-start | bytes 589832 | tf_op jit(solution)/shard_map/ppermute | solution.py:306
  231.7 22.0 %collective-permute-start.19 = (bf16[6,64,256]{2,1,0:T(8,128)(2,1)}, bf16[6,64,256]{2,1,0:T(8,128)(2,1)}, u32[]{:S(2)}, u32[]{:S(2)}) collective-permute-start(bf16[6,64,256]{2,1,0:T(8,128)(2,1)} %get-tuple-element.75), channel_id=1, source_target_pairs={{0,24},{4,28},{8,16},{12,20},{16,8},{20,12},{24,0},{28,4},{1,25},{... | collective-permute-start | bytes 589832 | tf_op jit(solution)/shard_map/ppermute | solution.py:306
  236.2 17.6 %collective-permute-start.20 = (bf16[6,64,256]{2,1,0:T(8,128)(2,1)}, bf16[6,64,256]{2,1,0:T(8,128)(2,1)}, u32[]{:S(2)}, u32[]{:S(2)}) collective-permute-start(bf16[6,64,256]{2,1,0:T(8,128)(2,1)} %get-tuple-element.76), channel_id=1, source_target_pairs={{0,28},{4,24},{8,20},{12,16},{16,12},{20,8},{24,4},{28,0},{1,29},{... | collective-permute-start | bytes 589832 | tf_op jit(solution)/shard_map/ppermute | solution.py:306
  253.5 375.5 %all-gather.5.cloned.1.call-start = ((), (), s32[]{:S(2)}) async-start(), calls=%async_computation.3 | async-start | bytes 7864320 | tf_op jit(solution)/shard_map/all_gather | solution.py:674
  308.1 31.7 %collective-permute-start.21 = (bf16[6,3,64,256]{3,2,1,0:T(8,128)(2,1)}, bf16[6,3,64,256]{3,2,1,0:T(8,128)(2,1)S(1)}, u32[]{:S(2)}, u32[]{:S(2)}) collective-permute-start(bf16[6,3,64,256]{3,2,1,0:T(8,128)(2,1)} %get-tuple-element.78), channel_id=1, source_target_pairs={{0,4},{4,0},{8,12},{12,8},{16,20},{20,16},{24,28},{28,24},{1,5},{5... | collective-permute-start | bytes 1769480 | tf_op jit(solution)/shard_map/ppermute | solution.py:306
  309.4 31.9 %collective-permute-start.22 = (bf16[6,3,64,256]{3,2,1,0:T(8,128)(2,1)}, bf16[6,3,64,256]{3,2,1,0:T(8,128)(2,1)S(1)}, u32[]{:S(2)}, u32[]{:S(2)}) collective-permute-start(bf16[6,3,64,256]{3,2,1,0:T(8,128)(2,1)} %get-tuple-element.79), channel_id=1, source_target_pairs={{0,8},{4,12},{8,0},{12,4},{16,24},{20,28},{24,16},{28,20},{1,9},{5... | collective-permute-start | bytes 1769480 | tf_op jit(solution)/shard_map/ppermute | solution.py:306
  335.8 25.5 %collective-permute-start.23 = (bf16[6,3,64,256]{3,2,1,0:T(8,128)(2,1)S(1)}, bf16[6,3,64,256]{3,2,1,0:T(8,128)(2,1)S(1)}, u32[]{:S(2)}, u32[]{:S(2)}) collective-permute-start(bf16[6,3,64,256]{3,2,1,0:T(8,128)(2,1)S(1)} %copy-done.27), channel_id=1, source_target_pairs={{0,12},{4,8},{8,4},{12,0},{16,28},{20,24},{24,20},{28,16},{1,13},{... | collective-permute-start | bytes 1769480 | tf_op jit(solution)/shard_map/ppermute | solution.py:306
  336.3 67.7 %collective-permute-start.24 = (bf16[6,3,64,256]{3,2,1,0:T(8,128)(2,1)S(1)}, bf16[6,3,64,256]{3,2,1,0:T(8,128)(2,1)S(1)}, u32[]{:S(2)}, u32[]{:S(2)}) collective-permute-start(bf16[6,3,64,256]{3,2,1,0:T(8,128)(2,1)S(1)} %copy-done.26), channel_id=1, source_target_pairs={{0,16},{4,20},{8,24},{12,28},{16,0},{20,4},{24,8},{28,12},{1,17},{... | collective-permute-start | bytes 1769480 | tf_op jit(solution)/shard_map/ppermute | solution.py:306
  337.0 80.3 %collective-permute-start.25 = (bf16[6,3,64,256]{3,2,1,0:T(8,128)(2,1)S(1)}, bf16[6,3,64,256]{3,2,1,0:T(8,128)(2,1)S(1)}, u32[]{:S(2)}, u32[]{:S(2)}) collective-permute-start(bf16[6,3,64,256]{3,2,1,0:T(8,128)(2,1)S(1)} %copy-done.25), channel_id=1, source_target_pairs={{0,20},{4,16},{8,28},{12,24},{16,4},{20,0},{24,12},{28,8},{1,21},{... | collective-permute-start | bytes 1769480 | tf_op jit(solution)/shard_map/ppermute | solution.py:306
  339.9 77.4 %collective-permute-start.26 = (bf16[6,3,64,256]{3,2,1,0:T(8,128)(2,1)S(1)}, bf16[6,3,64,256]{3,2,1,0:T(8,128)(2,1)S(1)}, u32[]{:S(2)}, u32[]{:S(2)}) collective-permute-start(bf16[6,3,64,256]{3,2,1,0:T(8,128)(2,1)S(1)} %copy-done.24), channel_id=1, source_target_pairs={{0,24},{4,28},{8,16},{12,20},{16,8},{20,12},{24,0},{28,4},{1,25},{... | collective-permute-start | bytes 1769480 | tf_op jit(solution)/shard_map/ppermute | solution.py:306
  341.3 76.0 %collective-permute-start.27 = (bf16[6,3,64,256]{3,2,1,0:T(8,128)(2,1)S(1)}, bf16[6,3,64,256]{3,2,1,0:T(8,128)(2,1)S(1)}, u32[]{:S(2)}, u32[]{:S(2)}) collective-permute-start(bf16[6,3,64,256]{3,2,1,0:T(8,128)(2,1)S(1)} %copy-done.23), channel_id=1, source_target_pairs={{0,28},{4,24},{8,20},{12,16},{16,12},{20,8},{24,4},{28,0},{1,29},{... | collective-permute-start | bytes 1769480 | tf_op jit(solution)/shard_map/ppermute | solution.py:306
  443.1 26.2 %collective-permute-start.28 = (bf16[2,768,1024]{2,1,0:T(8,128)(2,1)S(1)}, bf16[2,768,1024]{2,1,0:T(8,128)(2,1)S(1)}, u32[]{:S(2)}, u32[]{:S(2)}) collective-permute-start(bf16[2,768,1024]{2,1,0:T(8,128)(2,1)S(1)} %pad_maximum_fusion), channel_id=1, source_target_pairs={{0,1},{1,0},{2,3},{3,2},{4,5},{5,4},{6,7},{7,6},{8,9},{9,8},{10,11... | collective-permute-start | bytes 9437192 | tf_op jit(solution)/shard_map/ppermute | solution.py:323
  456.2 108.8 %collective-permute-start.56 = (bf16[4,128,768]{1,2,0:T(8,128)(2,1)}, bf16[4,128,768]{1,2,0:T(8,128)(2,1)}, u32[]{:S(2)}, u32[]{:S(2)}) collective-permute-start(bf16[4,128,768]{1,2,0:T(8,128)(2,1)} %pad_maximum_fusion.1), channel_id=1, source_target_pairs={{0,24},{4,28},{8,16},{12,20},{16,8},{20,12},{24,0},{28,4},{1,25},{... | collective-permute-start | bytes 2359304 | tf_op jit(solution)/shard_map/ppermute | solution.py:323
  470.0 35.5 %collective-permute-start.29 = (bf16[1,768,1024]{2,1,0:T(8,128)(2,1)S(1)}, bf16[1,768,1024]{2,1,0:T(8,128)(2,1)S(1)}, u32[]{:S(2)}, u32[]{:S(2)}) collective-permute-start(bf16[1,768,1024]{2,1,0:T(8,128)(2,1)S(1)} %fusion.27), channel_id=1, source_target_pairs={{0,2},{1,3},{2,0},{3,1},{4,6},{5,7},{6,4},{7,5},{8,10},{9,11},{10,... | collective-permute-start | bytes 4718600 | tf_op jit(solution)/shard_map/ppermute | solution.py:323
  473.5 63.3 %collective-permute-start.44 = (bf16[4,256,128]{2,1,0:T(8,128)(2,1)}, bf16[4,256,128]{2,1,0:T(8,128)(2,1)}, u32[]{:S(2)}, u32[]{:S(2)}) collective-permute-start(bf16[4,256,128]{2,1,0:T(8,128)(2,1)} %pad_maximum_fusion.13), channel_id=1, source_target_pairs={{0,4},{4,0},{8,12},{12,8},{16,20},{20,16},{24,28},{28,24},{1,5},{5... | collective-permute-start | bytes 786440 | tf_op jit(solution)/shard_map/ppermute | solution.py:323
  475.7 84.3 %collective-permute-start.47 = (bf16[4,128,640]{1,2,0:T(8,128)(2,1)}, bf16[4,128,640]{1,2,0:T(8,128)(2,1)}, u32[]{:S(2)}, u32[]{:S(2)}) collective-permute-start(bf16[4,128,640]{1,2,0:T(8,128)(2,1)} %pad_maximum_fusion.2), channel_id=1, source_target_pairs={{0,4},{4,0},{8,12},{12,8},{16,20},{20,16},{24,28},{28,24},{1,5},{5... | collective-permute-start | bytes 1966088 | tf_op jit(solution)/shard_map/ppermute | solution.py:323
  510.6 23.6 %collective-permute-start.54 = (f32[2,256]{1,0:T(2,128)S(1)}, f32[2,256]{1,0:T(2,128)S(1)}, u32[]{:S(2)}, u32[]{:S(2)}) collective-permute-start(f32[2,256]{1,0:T(2,128)S(1)} %pad_maximum_fusion.29), channel_id=1, source_target_pairs={{0,8},{4,12},{8,0},{12,4},{16,24},{20,28},{24,16},{28,20},{1,9},{5... | collective-permute-start | bytes 6152 | tf_op jit(solution)/shard_map/ppermute | solution.py:323
  533.8 27.5 %collective-permute-start.50 = (bf16[4,128,640]{1,2,0:T(8,128)(2,1)S(1)}, bf16[4,128,640]{1,2,0:T(8,128)(2,1)S(1)}, u32[]{:S(2)}, u32[]{:S(2)}) collective-permute-start(bf16[4,128,640]{1,2,0:T(8,128)(2,1)S(1)} %pad_maximum_fusion.3), channel_id=1, source_target_pairs={{0,8},{4,12},{8,0},{12,4},{16,24},{20,28},{24,16},{28,20},{1,9},{5... | collective-permute-start | bytes 1966088 | tf_op jit(solution)/shard_map/ppermute | solution.py:323
  534.2 16.8 %collective-permute-start.55 = (f32[1,256]{1,0:T(1,128)S(1)}, f32[1,256]{1,0:T(1,128)S(1)}, u32[]{:S(2)}, u32[]{:S(2)}) collective-permute-start(f32[1,256]{1,0:T(1,128)S(1)} %get-tuple-element.209), channel_id=1, source_target_pairs={{0,24},{4,28},{8,16},{12,20},{16,8},{20,12},{24,0},{28,4},{1,25},{... | collective-permute-start | bytes 3080 | tf_op jit(solution)/shard_map/ppermute | solution.py:323
  537.9 13.6 %collective-permute-start.45 = (bf16[2,256,128]{2,1,0:T(8,128)(2,1)S(1)}, bf16[2,256,128]{2,1,0:T(8,128)(2,1)S(1)}, u32[]{:S(2)}, u32[]{:S(2)}) collective-permute-start(bf16[2,256,128]{2,1,0:T(8,128)(2,1)S(1)} %pad_maximum_fusion.25), channel_id=1, source_target_pairs={{0,8},{4,12},{8,0},{12,4},{16,24},{20,28},{24,16},{28,20},{1,9},{5... | collective-permute-start | bytes 393224 | tf_op jit(solution)/shard_map/ppermute | solution.py:323
  561.2 14.4 %collective-permute-start.48 = (bf16[2,128,640]{1,2,0:T(8,128)(2,1)S(1)}, bf16[2,128,640]{1,2,0:T(8,128)(2,1)S(1)}, u32[]{:S(2)}, u32[]{:S(2)}) collective-permute-start(bf16[2,128,640]{1,2,0:T(8,128)(2,1)S(1)} %pad_maximum_fusion.8), channel_id=1, source_target_pairs={{0,8},{4,12},{8,0},{12,4},{16,24},{20,28},{24,16},{28,20},{1,9},{5... | collective-permute-start | bytes 983048 | tf_op jit(solution)/shard_map/ppermute | solution.py:323
  562.4 17.2 %collective-permute-start.51 = (bf16[2,128,640]{1,2,0:T(8,128)(2,1)S(1)}, bf16[2,128,640]{1,2,0:T(8,128)(2,1)S(1)}, u32[]{:S(2)}, u32[]{:S(2)}) collective-permute-start(bf16[2,128,640]{1,2,0:T(8,128)(2,1)S(1)} %pad_maximum_fusion.9), channel_id=1, source_target_pairs={{0,24},{4,28},{8,16},{12,20},{16,8},{20,12},{24,0},{28,4},{1,25},{... | collective-permute-start | bytes 983048 | tf_op jit(solution)/shard_map/ppermute | solution.py:323
  566.3 34.3 %collective-permute-start.57 = (bf16[2,128,768]{1,2,0:T(8,128)(2,1)S(1)}, bf16[2,128,768]{1,2,0:T(8,128)(2,1)S(1)}, u32[]{:S(2)}, u32[]{:S(2)}) collective-permute-start(bf16[2,128,768]{1,2,0:T(8,128)(2,1)S(1)} %pad_maximum_fusion.7), channel_id=1, source_target_pairs={{0,4},{4,0},{8,12},{12,8},{16,20},{20,16},{24,28},{28,24},{1,5},{5... | collective-permute-start | bytes 1179656 | tf_op jit(solution)/shard_map/ppermute | solution.py:323
  567.5 17.6 %collective-permute-start.38 = (bf16[4,256,128]{2,1,0:T(8,128)(2,1)S(1)}, bf16[4,256,128]{2,1,0:T(8,128)(2,1)S(1)}, u32[]{:S(2)}, u32[]{:S(2)}) collective-permute-start(bf16[4,256,128]{2,1,0:T(8,128)(2,1)S(1)} %pad_maximum_fusion.11), channel_id=1, source_target_pairs={{0,8},{4,12},{8,0},{12,4},{16,24},{20,28},{24,16},{28,20},{1,9},{5... | collective-permute-start | bytes 786440 | tf_op jit(solution)/shard_map/ppermute | solution.py:323
  568.8 20.5 %collective-permute-start.41 = (bf16[4,256,128]{2,1,0:T(8,128)(2,1)S(1)}, bf16[4,256,128]{2,1,0:T(8,128)(2,1)S(1)}, u32[]{:S(2)}, u32[]{:S(2)}) collective-permute-start(bf16[4,256,128]{2,1,0:T(8,128)(2,1)S(1)} %pad_maximum_fusion.12), channel_id=1, source_target_pairs={{0,24},{4,28},{8,16},{12,20},{16,8},{20,12},{24,0},{28,4},{1,25},{... | collective-permute-start | bytes 786440 | tf_op jit(solution)/shard_map/ppermute | solution.py:323
  575.7 18.1 %collective-permute-start.35 = (bf16[4,256,128]{2,1,0:T(8,128)(2,1)S(1)}, bf16[4,256,128]{2,1,0:T(8,128)(2,1)S(1)}, u32[]{:S(2)}, u32[]{:S(2)}) collective-permute-start(bf16[4,256,128]{2,1,0:T(8,128)(2,1)S(1)} %pad_maximum_fusion.10), channel_id=1, source_target_pairs={{0,4},{4,0},{8,12},{12,8},{16,20},{20,16},{24,28},{28,24},{1,5},{5... | collective-permute-start | bytes 786440 | tf_op jit(solution)/shard_map/ppermute | solution.py:323
  579.7 15.3 %collective-permute-start.49 = (bf16[1,128,640]{1,2,0:T(8,128)(2,1)S(1)}, bf16[1,128,640]{1,2,0:T(8,128)(2,1)S(1)}, u32[]{:S(2)}, u32[]{:S(2)}) collective-permute-start(bf16[1,128,640]{1,2,0:T(8,128)(2,1)S(1)} %fusion.44), channel_id=1, source_target_pairs={{0,24},{4,28},{8,16},{12,20},{16,8},{20,12},{24,0},{28,4},{1,25},{... | collective-permute-start | bytes 491528 | tf_op jit(solution)/shard_map/ppermute | solution.py:323
  585.1 15.4 %collective-permute-start.52 = (bf16[1,128,640]{1,2,0:T(8,128)(2,1)S(1)}, bf16[1,128,640]{1,2,0:T(8,128)(2,1)S(1)}, u32[]{:S(2)}, u32[]{:S(2)}) collective-permute-start(bf16[1,128,640]{1,2,0:T(8,128)(2,1)S(1)} %fusion.47), channel_id=1, source_target_pairs={{0,4},{4,0},{8,12},{12,8},{16,20},{20,16},{24,28},{28,24},{1,5},{5... | collective-permute-start | bytes 491528 | tf_op jit(solution)/shard_map/ppermute | solution.py:323
  601.6 18.7 %collective-permute-start.58 = (bf16[1,128,768]{1,2,0:T(8,128)(2,1)S(1)}, bf16[1,128,768]{1,2,0:T(8,128)(2,1)S(1)}, u32[]{:S(2)}, u32[]{:S(2)}) collective-permute-start(bf16[1,128,768]{1,2,0:T(8,128)(2,1)S(1)} %fusion.41), channel_id=1, source_target_pairs={{0,8},{4,12},{8,0},{12,4},{16,24},{20,28},{24,16},{28,20},{1,9},{5... | collective-permute-start | bytes 589832 | tf_op jit(solution)/shard_map/ppermute | solution.py:323
  (63 other events, 1169.0 us)
Sparse Core Ops, SparseCore 0:
  9.6 49.9 all-gather.2
  253.6 57.2 reduce-scatter.1
  510.7 66.4 all-gather.4
